TPU v7x, 128 devices: a whole 4x4x4 slice. The times are simulated.
128 devices in a mesh: fsdp: 16 (over z, x), ctx: 8 (over y, core).
Axes of the slice: x: 4, y: 4, z: 4, core: 2. Of those that a mesh axis runs over, the one named last changes fastest.
Arguments:
- inputs: bfloat16 [16, 1024, 1024], P('fsdp', 'ctx'), may hold values from -6 to 6
- mix_gain: bfloat16 [1024], P(('fsdp', 'ctx')), may hold values from 0.099609375 to 1.8984375
- in_proj: bfloat16 [1024, 3072], P(('fsdp', 'ctx')), may hold values from -0.1875 to 0.1875
- conv_kernel: bfloat16 [3, 1024], P(None, ('fsdp', 'ctx')), may hold values from -3 to 3
- out_proj: bfloat16 [1024, 1024], P(('fsdp', 'ctx')), may hold values from -0.1875 to 0.1875
- ffn_gain: bfloat16 [1024], P(('fsdp', 'ctx')), may hold values from 0.099609375 to 1.8984375
- gate_proj: bfloat16 [1024, 4608], P('fsdp', 'ctx'), may hold values from -0.1875 to 0.1875
- up_proj: bfloat16 [1024, 4608], P('fsdp', 'ctx'), may hold values from -0.1875 to 0.1875
- down_proj: bfloat16 [4608, 1024], P('ctx', 'fsdp'), may hold values from -0.09375 to 0.09375
- cotangent: bfloat16 [16, 1024, 1024], P('fsdp', 'ctx'), may hold values from -6 to 6
Outputs:
- block_out: bfloat16 [16, 1024, 1024], P('fsdp', 'ctx')
- grad_inputs: float32 [16, 1024, 1024], P('fsdp', 'ctx')
- grad_mix_gain: float32 [1024], P(('fsdp', 'ctx'))
- grad_in_proj: float32 [1024, 3072], P(('fsdp', 'ctx'))
- grad_conv_kernel: float32 [3, 1024], P(None, ('fsdp', 'ctx'))
- grad_out_proj: float32 [1024, 1024], P(('fsdp', 'ctx'))
- grad_ffn_gain: float32 [1024], P(('fsdp', 'ctx'))
- grad_gate_proj: float32 [1024, 4608], P('fsdp', 'ctx')
- grad_up_proj: float32 [1024, 4608], P('fsdp', 'ctx')
- grad_down_proj: float32 [4608, 1024], P('ctx', 'fsdp')
All inputs are finite; a program needn't handle non-finite values.
Results may differ from a plain program's by a relative error of at most 0.018.
Values may be sent and summed in bfloat16 or wider, within the bound.
A program may use at most 192 MiB of HBM per device.

v0:
```python
import jax
import jax.numpy as jnp
from jax import lax
from jax.sharding import PartitionSpec as P

epsilon = 1e-05


def from_behind(value, axis, steps):
    count = lax.axis_size(axis)
    initial, last = (max(0, -steps), min(count, count - steps))
    return lax.ppermute(value, axis, [(source, source + steps) for source in range(initial, last)])


def ffn_forward(rows_in, w_gate, w_up):
    gating = jnp.dot(rows_in, w_gate, preferred_element_type=jnp.float32)
    upward = jnp.dot(rows_in, w_up, preferred_element_type=jnp.float32)
    sigma = jax.nn.sigmoid(gating)
    activated = gating * sigma
    hidden = (activated * upward).astype(jnp.bfloat16)
    return (gating, upward, sigma, activated, hidden)


def ffn_backward(rows_in, rows_cot, w_gate, w_up, w_down, gating, upward, sigma, activated, hidden):
    d_hidden = jnp.dot(rows_cot, w_down.T, preferred_element_type=jnp.float32)
    grad_down = jnp.dot(hidden.T, rows_cot, preferred_element_type=jnp.float32)
    d_gating = (d_hidden * upward * sigma * (1.0 + gating * (1.0 - sigma))).astype(jnp.bfloat16)
    d_upward = (d_hidden * activated).astype(jnp.bfloat16)
    grad_gate = jnp.dot(rows_in.T, d_gating, preferred_element_type=jnp.float32)
    grad_up = jnp.dot(rows_in.T, d_upward, preferred_element_type=jnp.float32)
    d_second = jnp.dot(d_gating, w_gate.T, preferred_element_type=jnp.float32) + jnp.dot(
        d_upward, w_up.T, preferred_element_type=jnp.float32
    )
    return (d_second, grad_gate, grad_up, grad_down)


def per_device(
    inputs,
    mix_gain,
    in_proj,
    conv_kernel,
    out_proj,
    ffn_gain,
    gate_proj,
    up_proj,
    down_proj,
    cotangent,
):
    f32 = jnp.float32
    bf16 = jnp.bfloat16
    seq_count, block_len, width = inputs.shape
    fetched = (
        lax.all_gather(mix_gain, ("fsdp", "ctx"), axis=0, tiled=True),
        lax.all_gather(in_proj, ("fsdp", "ctx"), axis=0, tiled=True),
        lax.all_gather(conv_kernel, ("fsdp", "ctx"), axis=1, tiled=True),
        lax.all_gather(out_proj, ("fsdp", "ctx"), axis=0, tiled=True),
        lax.all_gather(ffn_gain, ("fsdp", "ctx"), axis=0, tiled=True),
    )
    gain_one, w_in, kernel, w_out, gain_two = fetched
    row_weights = (
        lax.all_gather(gate_proj, "fsdp", axis=0, tiled=True),
        lax.all_gather(up_proj, "fsdp", axis=0, tiled=True),
        lax.all_gather(down_proj, "fsdp", axis=1, tiled=True),
    )
    flat_in = inputs.astype(f32).reshape(-1, width)
    scale_one = lax.rsqrt(jnp.mean(flat_in * flat_in, axis=-1, keepdims=True) + epsilon)
    normed_one = flat_in * scale_one
    lifted = (normed_one * gain_one.astype(f32)).astype(bf16)
    projected = jnp.dot(lifted, w_in, preferred_element_type=f32)
    b_part = projected[:, :width]
    c_part = projected[:, width : 2 * width]
    x_part = projected[:, 2 * width :]
    carried = (b_part * x_part).astype(bf16).reshape(seq_count, block_len, width)
    before = from_behind(carried[:, -2:, :], "ctx", 1)
    extended = jnp.concatenate([before, carried], 1).astype(f32)
    taps = kernel.astype(f32)
    mixed = taps[0] * extended[:, :-2] + taps[1] * extended[:, 1:-1] + taps[2] * extended[:, 2:]
    mixed = mixed.reshape(-1, width)
    gated = (c_part * mixed).astype(bf16)
    middle = flat_in + jnp.dot(gated, w_out, preferred_element_type=f32)
    scale_two = lax.rsqrt(jnp.mean(middle * middle, axis=-1, keepdims=True) + epsilon)
    normed_two = middle * scale_two
    second_in = (normed_two * gain_two.astype(f32)).astype(bf16)
    flat_cot = cotangent.reshape(-1, width)
    w_gate, w_up, w_down = (
        lax.all_gather(row_weights[0], "ctx", axis=1, tiled=True),
        lax.all_gather(row_weights[1], "ctx", axis=1, tiled=True),
        lax.all_gather(row_weights[2], "ctx", axis=0, tiled=True),
    )
    gating, upward, sigma, activated, hidden = ffn_forward(second_in, w_gate, w_up)
    result = middle + jnp.dot(hidden, w_down, preferred_element_type=f32)
    d_second, grad_gate, grad_up, grad_down = ffn_backward(
        second_in, flat_cot, w_gate, w_up, w_down, gating, upward, sigma, activated, hidden
    )
    ffn_terms = (
        lax.psum_scatter(
            grad_gate.astype(jnp.bfloat16), "ctx", scatter_dimension=1, tiled=True
        ).astype(jnp.float32),
        lax.psum_scatter(
            grad_up.astype(jnp.bfloat16), "ctx", scatter_dimension=1, tiled=True
        ).astype(jnp.float32),
        lax.psum_scatter(
            grad_down.astype(jnp.bfloat16), "ctx", scatter_dimension=0, tiled=True
        ).astype(jnp.float32),
    )
    block_out = result.astype(bf16).reshape(seq_count, block_len, width)
    ffn_owned = (
        lax.psum_scatter(
            ffn_terms[0].astype(jnp.bfloat16), "fsdp", scatter_dimension=0, tiled=True
        ).astype(jnp.float32),
        lax.psum_scatter(
            ffn_terms[1].astype(jnp.bfloat16), "fsdp", scatter_dimension=0, tiled=True
        ).astype(jnp.float32),
        lax.psum_scatter(
            ffn_terms[2].astype(jnp.bfloat16), "fsdp", scatter_dimension=1, tiled=True
        ).astype(jnp.float32),
    )
    grad_gain_two = jnp.sum(d_second * normed_two, axis=0)
    scaled_two = d_second * gain_two.astype(f32)
    d_middle = flat_cot.astype(f32) + scale_two * (
        scaled_two - normed_two * jnp.mean(scaled_two * normed_two, axis=-1, keepdims=True)
    )
    d_branch = d_middle.astype(bf16)
    d_gated = jnp.dot(d_branch, w_out.T, preferred_element_type=f32)
    grad_out = jnp.dot(gated.T, d_branch, preferred_element_type=f32)
    d_mixed = (d_gated * c_part).reshape(seq_count, block_len, width)
    d_cpart = d_gated * mixed
    after = from_behind(d_mixed[:, :2, :], "ctx", -1)
    d_extended = jnp.concatenate([d_mixed, after], 1)
    d_carried = (
        taps[2] * d_extended[:, :-2] + taps[1] * d_extended[:, 1:-1] + taps[0] * d_extended[:, 2:]
    )
    grad_kernel = jnp.stack(
        [
            jnp.sum(d_mixed * extended[:, :-2], axis=(0, 1)),
            jnp.sum(d_mixed * extended[:, 1:-1], axis=(0, 1)),
            jnp.sum(d_mixed * extended[:, 2:], axis=(0, 1)),
        ],
        0,
    )
    d_carried = d_carried.reshape(-1, width)
    d_projected = jnp.concatenate([d_carried * x_part, d_cpart, d_carried * b_part], -1).astype(
        bf16
    )
    d_lifted = jnp.dot(d_projected, w_in.T, preferred_element_type=f32)
    grad_in = jnp.dot(lifted.T, d_projected, preferred_element_type=f32)
    grad_gain_one = jnp.sum(d_lifted * normed_one, axis=0)
    scaled_one = d_lifted * gain_one.astype(f32)
    d_inputs = d_middle + scale_one * (
        scaled_one - normed_one * jnp.mean(scaled_one * normed_one, axis=-1, keepdims=True)
    )
    grad_inputs = d_inputs.reshape(seq_count, block_len, width)
    owned = (
        lax.psum_scatter(grad_gain_one, ("fsdp", "ctx"), scatter_dimension=0, tiled=True),
        lax.psum_scatter(grad_in, ("fsdp", "ctx"), scatter_dimension=0, tiled=True),
        lax.psum_scatter(grad_kernel, ("fsdp", "ctx"), scatter_dimension=1, tiled=True),
        lax.psum_scatter(grad_out, ("fsdp", "ctx"), scatter_dimension=0, tiled=True),
        lax.psum_scatter(grad_gain_two, ("fsdp", "ctx"), scatter_dimension=0, tiled=True),
    )
    return (
        block_out,
        grad_inputs,
        owned[0],
        owned[1],
        owned[2],
        owned[3],
        owned[4],
        ffn_owned[0],
        ffn_owned[1],
        ffn_owned[2],
    )


def solution(mesh):
    in_specs = (
        P("fsdp", "ctx", None),
        P(("fsdp", "ctx")),
        P(("fsdp", "ctx"), None),
        P(None, ("fsdp", "ctx")),
        P(("fsdp", "ctx"), None),
        P(("fsdp", "ctx")),
        P("fsdp", "ctx"),
        P("fsdp", "ctx"),
        P("ctx", "fsdp"),
        P("fsdp", "ctx", None),
    )
    out_specs = (
        P("fsdp", "ctx", None),
        P("fsdp", "ctx", None),
        P(("fsdp", "ctx")),
        P(("fsdp", "ctx"), None),
        P(None, ("fsdp", "ctx")),
        P(("fsdp", "ctx"), None),
        P(("fsdp", "ctx")),
        P("fsdp", "ctx"),
        P("fsdp", "ctx"),
        P("ctx", "fsdp"),
    )
    return jax.shard_map(
        per_device, mesh=mesh, in_specs=in_specs, out_specs=out_specs, check_vma=False
    )
```

profile of v0, /device:TPU:1, one launch (start us, length us, event | category | flops | bytes accessed | tf_op | source)
XLA Modules:
  0.0 1740.7 jit_solution(9173308502073530897)
XLA Ops:
  10.6 45.4 %all-gather.14.cloned.1.call-done = bf16[1024,576]{1,0:T(8,128)(2,1)} async-done(((bf16[64,576]{1,0:T(8,128)(2,1)}), bf16[1024,576]{1,0:T(8,128)(2,1)}) %all-gather.14.cloned.1.call-update) | async-done | bytes 1179664 | tf_op jit(solution)/shard_map/all_gather | solution.py:61
  58.5 42.6 %all-gather.18.cloned.1.call-done = bf16[1024,576]{1,0:T(8,128)(2,1)} async-done(((bf16[64,576]{1,0:T(8,128)(2,1)}), bf16[1024,576]{1,0:T(8,128)(2,1)}) %all-gather.18.cloned.1.call-update) | async-done | bytes 1179664 | tf_op jit(solution)/shard_map/all_gather | solution.py:62
  103.7 42.5 %all-gather.22.cloned.1.call-done = bf16[576,1024]{0,1:T(8,128)(2,1)} async-done(((bf16[576,64]{0,1:T(8,128)(2,1)}), bf16[576,1024]{0,1:T(8,128)(2,1)}) %all-gather.22.cloned.1.call-update) | async-done | bytes 1179664 | tf_op jit(solution)/shard_map/all_gather | solution.py:63
  149.1 66.0 %all-reduce.6 = (bf16[1024]{0:T(1024)(128)(2,1)S(1)}, bf16[1024]{0:T(1024)(128)(2,1)S(1)}) all-reduce(bf16[1024]{0:T(1024)(128)(2,1)S(1)} %dynamic-update-slice, bf16[1024]{0:T(1024)(128)(2,1)S(1)} %dynamic-update-slice.1), channel_id=1, replica_groups=mesh['fsdp'=16,'ctx'=8] {'fsdp','ctx'}, use_global_device_ids=true, to_apply=%add | all-reduce | flops 2048 | bytes 8192
  215.1 34.1 %all-gather = bf16[128,8,3]{1,2,0:T(4,128)(2,1)S(1)} all-gather(bf16[1,8,3]{1,2,0:T(4,128)(2,1)S(1)} %bitcast.94), channel_id=1, replica_groups=mesh['fsdp'=16,'ctx'=8] {'fsdp','ctx'}, dimensions={0}, use_global_device_ids=true | all-gather | bytes 6192 | tf_op jit(solution)/shard_map/all_gather | solution.py:55
  257.8 26.8 %all-gather.12.cloned.1.call-done = bf16[1024,1024]{1,0:T(8,128)(2,1)} async-done(((bf16[8,1024]{1,0:T(8,128)(2,1)}), bf16[1024,1024]{1,0:T(8,128)(2,1)}) %all-gather.12.cloned.1.call-update) | async-done | bytes 2097168 | tf_op jit(solution)/shard_map/all_gather | solution.py:56
  286.8 50.9 %all-gather.16.cloned.1.call-done = bf16[1024,4608]{0,1:T(8,128)(2,1)} async-done(((bf16[1024,576]{0,1:T(8,128)(2,1)}), bf16[1024,4608]{0,1:T(8,128)(2,1)}) %all-gather.16.cloned.1.call-update) | async-done | bytes 9437200 | tf_op jit(solution)/shard_map/all_gather | solution.py:86
  337.7 8.3 fusion.42
  346.0 47.8 %all-gather.20.cloned.1.call-done = bf16[1024,4608]{0,1:T(8,128)(2,1)} async-done(((bf16[1024,576]{0,1:T(8,128)(2,1)}), bf16[1024,4608]{0,1:T(8,128)(2,1)}) %all-gather.20.cloned.1.call-update) | async-done | bytes 9437200 | tf_op jit(solution)/shard_map/all_gather | solution.py:87
  393.8 8.3 fusion.43
  402.0 47.8 %all-gather.24.cloned.1.call-done = bf16[4608,1024]{1,0:T(8,128)(2,1)} async-done(((bf16[576,1024]{1,0:T(8,128)(2,1)}), bf16[4608,1024]{1,0:T(8,128)(2,1)}) %all-gather.24.cloned.1.call-update) | async-done | bytes 9437200 | tf_op jit(solution)/shard_map/all_gather | solution.py:88
  449.8 10.1 multiply_convert_fusion
  466.1 6.4 convolution_convert_fusion.1
  472.5 6.4 convolution_convert_fusion
  479.2 43.7 %reduce-scatter.20.cloned.1.call-done = bf16[1024,576]{0,1:T(8,128)(2,1)} async-done(((bf16[1024,4608]{0,1:T(8,128)(2,1)}), bf16[1024,576]{0,1:T(8,128)(2,1)}) %reduce-scatter.20.cloned.1.call-update) | async-done | bytes 1179664 | tf_op jit(solution)/shard_map/reduce_scatter | solution.py:96
  525.3 56.8 %reduce-scatter.22.cloned.1.call-done = bf16[1024,576]{0,1:T(8,128)(2,1)} async-done(((bf16[1024,4608]{0,1:T(8,128)(2,1)}), bf16[1024,576]{0,1:T(8,128)(2,1)}) %reduce-scatter.22.cloned.1.call-update) | async-done | bytes 1179664 | tf_op jit(solution)/shard_map/reduce_scatter | solution.py:99
  584.7 57.0 %reduce-scatter.24.cloned.1.call-done = bf16[576,1024]{1,0:T(8,128)(2,1)} async-done(((bf16[4608,1024]{1,0:T(8,128)(2,1)}), bf16[576,1024]{1,0:T(8,128)(2,1)}) %reduce-scatter.24.cloned.1.call-update) | async-done | bytes 1179664 | tf_op jit(solution)/shard_map/reduce_scatter | solution.py:102
  667.5 6.4 fusion.23
  674.0 6.3 fusion.2
  682.7 65.8 %all-reduce.5 = (f32[1024]{0:T(1024)S(1)}, f32[3,1024]{1,0:T(4,128)S(1)}, f32[1024]{0:T(1024)S(1)}) all-reduce(f32[1024]{0:T(1024)S(1)} %get-tuple-element.65, f32[3,1024]{1,0:T(4,128)S(1)} %pad_maximum_fusion.4, f32[1024]{0:T(1024)S(1)} %get-tuple-element.63), channel_id=2, replica_groups=mesh['fsdp'=16,'ctx'=8] {'fsdp','ctx'}, use_global_device_ids=true, to_apply=%region_5.0.clone | all-reduce | flops 5120 | bytes 40960
  753.2 39.4 %reduce-scatter.28.cloned.1.call-done = bf16[64,576]{1,0:T(8,128)(2,1)} async-done(((bf16[1024,576]{1,0:T(8,128)(2,1)}), bf16[64,576]{1,0:T(8,128)(2,1)}) %reduce-scatter.28.cloned.1.call-update) | async-done | bytes 73744
  794.4 73.8 %reduce-scatter.30.cloned.1.call-done = bf16[64,576]{1,0:T(8,128)(2,1)} async-done(((bf16[1024,576]{1,0:T(8,128)(2,1)}), bf16[64,576]{1,0:T(8,128)(2,1)}) %reduce-scatter.30.cloned.1.call-update) | async-done | bytes 73744
  870.1 637.5 %reduce-scatter.18.cloned.1.call-done = f32[8,1024]{1,0:T(8,128)} async-done(((f32[1024,1024]{1,0:T(8,128)}), f32[8,1024]{1,0:T(8,128)}) %reduce-scatter.18.cloned.1.call-update) | async-done | bytes 32784 | tf_op jit(solution)/shard_map/reduce_scatter | solution.py:157
  1507.6 226.6 %reduce-scatter.16.cloned.1.call-done = f32[8,3072]{1,0:T(8,128)} async-done(((f32[1024,3072]{1,0:T(8,128)}), f32[8,3072]{1,0:T(8,128)}) %reduce-scatter.16.cloned.1.call-update) | async-done | bytes 98320 | tf_op jit(solution)/shard_map/reduce_scatter | solution.py:155
  (127 shorter events, 69.9 us)
Async XLA Ops:
  7.2 48.8 %all-gather.14.cloned.1.call-start = ((), (), s32[]{:S(2)}) async-start(), calls=%async_computation.10 | async-start | bytes 1392640 | tf_op jit(solution)/shard_map/all_gather | solution.py:61
  7.9 93.2 %all-gather.18.cloned.1.call-start = ((), (), s32[]{:S(2)}) async-start(), calls=%async_computation.12 | async-start | bytes 1392640 | tf_op jit(solution)/shard_map/all_gather | solution.py:62
  8.7 137.5 %all-gather.22.cloned.1.call-start = ((), (), s32[]{:S(2)}) async-start(), calls=%async_computation.14 | async-start | bytes 1392640 | tf_op jit(solution)/shard_map/all_gather | solution.py:63
  9.4 240.3 %all-gather.10.cloned.1.call-start = ((), (), s32[]{:S(2)}) async-start(), calls=%async_computation.8 | async-start | bytes 6340608 | tf_op jit(solution)/shard_map/all_gather | solution.py:54
  10.0 274.6 %all-gather.12.cloned.1.call-start = ((), (), s32[]{:S(2)}) async-start(), calls=%async_computation.9 | async-start | bytes 2113536 | tf_op jit(solution)/shard_map/all_gather | solution.py:56
  10.6 327.1 %all-gather.16.cloned.1.call-start = ((), (), s32[]{:S(2)}) async-start(), calls=%async_computation.11 | async-start | bytes 10616832 | tf_op jit(solution)/shard_map/all_gather | solution.py:86
  58.5 335.3 %all-gather.20.cloned.1.call-start = ((), (), s32[]{:S(2)}) async-start(), calls=%async_computation.13 | async-start | bytes 10616832 | tf_op jit(solution)/shard_map/all_gather | solution.py:87
  103.6 45.1 %copy-start.15 = (bf16[8]{0:T(256)(128)(2,1)S(1)}, bf16[8]{0:T(256)(128)(2,1)}, u32[]{:S(2)}) copy-start(bf16[8]{0:T(256)(128)(2,1)} %param.11) | copy-start | bytes 52
  103.6 45.3 %copy-start.16 = (bf16[8]{0:T(256)(128)(2,1)S(1)}, bf16[8]{0:T(256)(128)(2,1)}, u32[]{:S(2)}) copy-start(bf16[8]{0:T(256)(128)(2,1)} %param.15) | copy-start | bytes 52
  103.6 111.5 %copy-start.14 = (bf16[3,8]{1,0:T(4,128)(2,1)S(1)}, bf16[3,8]{1,0:T(4,128)(2,1)}, u32[]{:S(2)}) copy-start(bf16[3,8]{1,0:T(4,128)(2,1)} %param.13) | copy-start | bytes 148
  103.6 146.0 %copy-start = (bf16[1,128,1024]{2,1,0:T(8,128)(2,1)S(1)}, bf16[1,128,1024]{2,1,0:T(8,128)(2,1)}, u32[]{:S(2)}) copy-start(bf16[1,128,1024]{2,1,0:T(8,128)(2,1)} %param.10) | copy-start | bytes 786436
  103.6 346.2 %all-gather.24.cloned.1.call-start = ((), (), s32[]{:S(2)}) async-start(), calls=%async_computation.15 | async-start | bytes 10616832 | tf_op jit(solution)/shard_map/all_gather | solution.py:88
  148.6 374.3 %reduce-scatter.20.cloned.1.call-start = ((), (), s32[]{:S(2)}) async-start(), calls=%async_computation.18 | async-start | bytes 10616832 | tf_op jit(solution)/shard_map/reduce_scatter | solution.py:96
  253.7 3.1 collective-permute-start
  257.8 28.9 %copy-start.3 = (bf16[128,1024]{1,0:T(8,128)(2,1)}, bf16[128,1024]{1,0:T(8,128)(2,1)S(1)}, u32[]{:S(2)}) copy-start(bf16[128,1024]{1,0:T(8,128)(2,1)S(1)} %get-tuple-element.75) | copy-start | bytes 786436
  346.0 103.9 %copy-start.6 = (bf16[1,128,1024]{2,1,0:T(8,128)(2,1)S(1)}, bf16[1,128,1024]{2,1,0:T(8,128)(2,1)}, u32[]{:S(2)}) copy-start(bf16[1,128,1024]{2,1,0:T(8,128)(2,1)} %param.19) | copy-start | bytes 786436
  466.1 116.1 %reduce-scatter.22.cloned.1.call-start = ((), (), s32[]{:S(2)}) async-start(), calls=%async_computation.19 | async-start | bytes 10616832 | tf_op jit(solution)/shard_map/reduce_scatter | solution.py:99
  472.5 169.1 %reduce-scatter.24.cloned.1.call-start = ((), (), s32[]{:S(2)}) async-start(), calls=%async_computation.20 | async-start | bytes 10616832 | tf_op jit(solution)/shard_map/reduce_scatter | solution.py:102
  478.9 272.5 %reduce-scatter.26.cloned.1.call-start = ((), (), s32[]{:S(2)}) async-start(), calls=%async_computation.21 | async-start | bytes 1392640
  525.3 267.3 %reduce-scatter.28.cloned.1.call-start = ((), (), s32[]{:S(2)}) async-start(), calls=%async_computation.22 | async-start | bytes 1392640
  584.6 283.6 %reduce-scatter.30.cloned.1.call-start = ((), (), s32[]{:S(2)}) async-start(), calls=%async_computation.23 | async-start | bytes 1392640
  644.1 863.5 %reduce-scatter.18.cloned.1.call-start = ((), (), s32[]{:S(2)}) async-start(), calls=%async_computation.17 | async-start | bytes 4227072 | tf_op jit(solution)/shard_map/reduce_scatter | solution.py:157
  658.2 1076.0 %reduce-scatter.16.cloned.1.call-start = ((), (), s32[]{:S(2)}) async-start(), calls=%async_computation.16 | async-start | bytes 12681216 | tf_op jit(solution)/shard_map/reduce_scatter | solution.py:155
  660.9 5.4 collective-permute-start.1
  (13 other events, 57.6 us)
Sparse Core Ops, SparseCore 0:
  10.1 45.8 all-gather.13
  58.1 42.8 all-gather.17
  103.2 42.8 all-gather.21
  149.1 69.0 all-gather.9
  221.3 63.2 all-gather.11
  286.1 51.5 all-gather.15
  339.4 54.3 all-gather.19
  395.4 54.3 all-gather.23
  466.2 56.6 reduce-scatter.19
  525.1 57.0 reduce-scatter.21
  584.6 57.0 reduce-scatter.23
  644.7 72.0 reduce-scatter.25
  720.0 72.5 reduce-scatter.27
  795.7 72.5 reduce-scatter.29
  871.0 636.5 reduce-scatter.17
  1513.8 220.3 reduce-scatter.15
where the time goes:
time: 1740 us
  waiting for transfers between devices  1440 us (83%)
  blocking collectives  166 us (10%)
  matrix products  81.6 us (5%)
  local copies, waits for them, and re-layouts  24.6 us (1%)
    reduce_scatter x1, waiting for transfers between devices, per_device(): lax.psum_scatter(grad_out, ('fsdp', 'ctx'), scatter_dimension=0, tiled=True)  638 us
    reduce_scatter x1, waiting for transfers between devices, per_device(): lax.psum_scatter(grad_in, ('fsdp', 'ctx'), scatter_dimension=0, tiled=True)  227 us
    unnamed x2, blocking collectives  132 us
    unnamed x19, waiting for transfers between devices  116 us
    reduce_scatter x1, waiting for transfers between devices, per_device(): lax.psum_scatter(grad_down.astype(jnp.bfloat16), 'ctx', scatter_dimension...  57 us
    reduce_scatter x1, waiting for transfers between devices, per_device(): lax.psum_scatter(grad_up.astype(jnp.bfloat16), 'ctx', scatter_dimension=1...  56.8 us
    all_gather x1, waiting for transfers between devices, per_device(): lax.all_gather(row_weights[0], 'ctx', axis=1, tiled=True)  50.9 us
    all_gather x1, waiting for transfers between devices, per_device(): lax.all_gather(row_weights[1], 'ctx', axis=1, tiled=True)  47.8 us
  transfers between devices with their start and end apart: 18, of which 16 were waited for; matrix products, arithmetic and copies ran while one was open for 5% of the time, Pallas kernels for 0%

commit v1 on v0

v1 whole, which is shorter than its diff:
```python
import jax
import jax.numpy as jnp
from jax import lax
from jax.experimental import pallas as pl
from jax.experimental.pallas import tpu as pltpu
from jax.sharding import PartitionSpec as P

epsilon = 1e-05
f32 = jnp.float32
bf16 = jnp.bfloat16
MESH = pl.DeviceIdType.MESH

GU = 1152
FFL = 1792
HID = 640
CR = 80
CL = 512


def mm(a, b):
    return lax.dot_general(a, b, (((1,), (0,)), ((), ())), preferred_element_type=f32)


def mt(a, b):
    return lax.dot_general(a, b, (((1,), (1,)), ((), ())), preferred_element_type=f32)


def tm(a, b):
    return lax.dot_general(a, b, (((0,), (0,)), ((), ())), preferred_element_type=f32)


def add_into(ref, *others):
    total = ref[...].astype(f32)
    for other in others:
        total = total + other[...].astype(f32)
    ref[...] = total.astype(ref.dtype)


class Link:
    def __init__(self, send_sems, recv_sems):
        self.send_sems, self.recv_sems = send_sems, recv_sems
        self.used = 0
        self.started = []

    def reserve(self, count):
        first = self.used
        self.used += count
        return first

    def copy(self, src, dst, device, slot):
        return pltpu.make_async_remote_copy(
            src_ref=src,
            dst_ref=dst,
            send_sem=self.send_sems.at[slot],
            recv_sem=self.recv_sems.at[slot],
            device_id=device,
            device_id_type=MESH,
        )

    def send(self, src, dst, device):
        slot = self.reserve(1)
        self.copy(src, dst, device, slot).start()
        self.started.append((src, device, slot))
        return (device, slot)

    def landed(self, handle, ref):
        device, slot = handle
        self.copy(ref, ref, device, slot).wait_recv()

    def drain(self):
        for src, device, slot in self.started:
            self.copy(src, src, device, slot).wait_send()


def ring(value, step):
    return lax.rem(value + step, 4)


class RingGather:
    def __init__(self, link, view, me, plus, minus):
        self.link, self.view, self.me, self.plus, self.minus = link, view, me, plus, minus

    def start(self):
        own = self.view(self.me, None)
        self.hp = self.link.send(own, own, self.plus)
        self.hm = self.link.send(own, own, self.minus)

    def forward(self):
        left, right = ring(self.me, 3), ring(self.me, 1)
        self.link.landed(self.hp, self.view(left, None))
        part = self.view(left, 0)
        self.fp = self.link.send(part, part, self.plus)
        self.link.landed(self.hm, self.view(right, None))
        part = self.view(right, 1)
        self.fm = self.link.send(part, part, self.minus)

    def finish(self):
        far = ring(self.me, 2)
        self.link.landed(self.fp, self.view(far, 0))
        self.link.landed(self.fm, self.view(far, 1))


class RingScatter:
    def __init__(self, link, view, me, plus, minus, r1a, r1b, r2a, r2b):
        self.link, self.view, self.me, self.plus, self.minus = link, view, me, plus, minus
        self.r1a, self.r1b, self.r2a, self.r2b = r1a, r1b, r2a, r2b

    def start(self):
        far = ring(self.me, 2)
        self.h1a = self.link.send(self.view(far, 0), self.r1a, self.plus)
        self.h1b = self.link.send(self.view(far, 1), self.r1b, self.minus)

    def middle(self):
        left, right = ring(self.me, 3), ring(self.me, 1)
        self.link.landed(self.h1a, self.r1a)
        add_into(self.view(right, 0), self.r1a)
        self.h2a = self.link.send(self.view(right, None), self.r2a, self.plus)
        self.link.landed(self.h1b, self.r1b)
        add_into(self.view(left, 1), self.r1b)
        self.h2b = self.link.send(self.view(left, None), self.r2b, self.minus)

    def finish(self):
        self.link.landed(self.h2a, self.r2a)
        self.link.landed(self.h2b, self.r2b)
        add_into(self.view(self.me, None), self.r2a, self.r2b)


class CtxGather:
    def __init__(self, link, buf, y, core, plus, minus, other):
        self.link, self.buf, self.y, self.core = link, buf, y, core
        self.plus, self.minus, self.other = plus, minus, other

    def half(self, which, part):
        return self.buf.at[which, self.core, pl.ds(64 * part, 64)]

    def start(self):
        own = self.buf.at[self.y, self.core]
        self.hp = self.link.send(own, own, self.plus)
        self.hm = self.link.send(own, own, self.minus)
        self.ho = [self.link.send(own, own, self.other)]

    def forward(self):
        left, right = ring(self.y, 3), ring(self.y, 1)
        block = self.buf.at[left, self.core]
        self.link.landed(self.hp, block)
        self.fp = self.link.send(self.half(left, 0), self.half(left, 0), self.plus)
        self.ho.append(self.link.send(block, block, self.other))
        block = self.buf.at[right, self.core]
        self.link.landed(self.hm, block)
        self.fm = self.link.send(self.half(right, 1), self.half(right, 1), self.minus)
        self.ho.append(self.link.send(block, block, self.other))

    def across(self):
        far = ring(self.y, 2)
        self.link.landed(self.fp, self.half(far, 0))
        self.link.landed(self.fm, self.half(far, 1))
        block = self.buf.at[far, self.core]
        self.ho.append(self.link.send(block, block, self.other))

    def finish(self):
        for handle, step in zip(self.ho, (0, 3, 1, 2)):
            self.link.landed(handle, self.buf.at[ring(self.y, step), 1 - self.core])


class CtxScatter:
    def __init__(self, link, part, rb, r1, r2, y, core, plus, minus, other):
        self.link, self.part, self.rb, self.r1, self.r2 = link, part, rb, r1, r2
        self.y, self.core = y, core
        self.plus, self.minus, self.other = plus, minus, other
        self.first = link.reserve(4)

    def group(self, step):
        return lax.rem(self.y + 2 + step + step // 2 + 2 * (step // 3), 4)

    def cross(self, step):
        g = self.group(step)
        self.link.copy(
            self.part.at[g, 1 - self.core], self.rb.at[g], self.other, self.first + step
        ).start()

    def crossed(self, g, step):
        ref = self.rb.at[g]
        self.link.copy(ref, ref, self.other, self.first + step).wait_recv()

    def start(self):
        far = ring(self.y, 2)
        self.crossed(far, 0)
        block = self.part.at[far, self.core]
        add_into(block, self.rb.at[far])
        self.h1a = self.link.send(block.at[pl.ds(0, 64)], self.r1.at[0], self.plus)
        self.h1b = self.link.send(block.at[pl.ds(64, 64)], self.r1.at[1], self.minus)

    def middle(self):
        left, right = ring(self.y, 3), ring(self.y, 1)
        self.crossed(left, 1)
        self.crossed(right, 2)
        block = self.part.at[right, self.core]
        self.link.landed(self.h1a, self.r1.at[0])
        add_into(block.at[pl.ds(0, 64)], self.rb.at[right, pl.ds(0, 64)], self.r1.at[0])
        add_into(block.at[pl.ds(64, 64)], self.rb.at[right, pl.ds(64, 64)])
        self.h2a = self.link.send(block, self.r2.at[0], self.plus)
        block = self.part.at[left, self.core]
        self.link.landed(self.h1b, self.r1.at[1])
        add_into(block.at[pl.ds(0, 64)], self.rb.at[left, pl.ds(0, 64)])
        add_into(block.at[pl.ds(64, 64)], self.rb.at[left, pl.ds(64, 64)], self.r1.at[1])
        self.h2b = self.link.send(block, self.r2.at[1], self.minus)

    def finish(self):
        self.crossed(self.y, 3)
        self.link.landed(self.h2a, self.r2.at[0])
        self.link.landed(self.h2b, self.r2.at[1])
        return (
            self.part[self.y, self.core].astype(f32)
            + self.rb[self.y].astype(f32)
            + self.r2[0].astype(f32)
            + self.r2[1].astype(f32)
        )

    def drain(self):
        for step in range(4):
            g = self.group(step)
            src = self.part.at[g, 1 - self.core]
            self.link.copy(src, src, self.other, self.first + step).wait_send()


def block_kernel(
    x_ref,
    cot_ref,
    wff_ref,
    win_ref,
    wout_ref,
    pack_ref,
    out_ref,
    gin_ref,
    gff_ref,
    gwin_ref,
    gwout_ref,
    gpack_ref,
    send_sems,
    recv_sems,
    xg,
    cotg,
    h2g,
    dg,
    wf,
    wc,
    pre_in,
    pre_pack,
    w_in,
    w_out,
    h1g,
    scale_g,
    proj,
    bx_pad,
    z_buf,
    y_buf,
    hid_buf,
    dgu_buf,
    dz_pad,
    dp_buf,
    mix_acc,
    rs_part,
    rs_rb,
    rs_r1,
    rs_r2,
    gf,
    gc,
    gf_a1,
    gf_a2,
    gf_b1,
    gf_b2,
    gf_a3,
    gf_a4,
    gf_b3,
    gf_b4,
    gc_a1,
    gc_a2,
    gc_b1,
    gc_b2,
    gc_a3,
    gc_a4,
    gc_b3,
    gc_b4,
    post_send,
    post_in,
    post_own,
    post_pack,
):
    f = lax.axis_index("fsdp")
    c = lax.axis_index("ctx")
    z, x = f // 4, lax.rem(f, 4)
    y, core = c // 2, lax.rem(c, 2)
    y_plus, y_minus = (f, ring(y, 1) * 2 + core), (f, ring(y, 3) * 2 + core)
    other = (f, y * 2 + 1 - core)
    x_plus, x_minus = (z * 4 + ring(x, 1), c), (z * 4 + ring(x, 3), c)
    z_plus, z_minus = (ring(z, 1) * 4 + x, c), (ring(z, 3) * 4 + x, c)
    mates = [(f, lax.rem(c + step, 8)) for step in range(1, 8)]

    barrier = pltpu.get_barrier_semaphore()
    for device in mates + [x_plus, x_minus, z_plus, z_minus]:
        pl.semaphore_signal(barrier, inc=1, device_id=device, device_id_type=MESH)
    pl.semaphore_wait(barrier, 11)

    link = Link(send_sems, recv_sems)

    def ctx_gather(buf):
        return CtxGather(link, buf, y, core, y_plus, y_minus, other)

    def ctx_scatter(n):
        return CtxScatter(
            link, rs_part.at[n], rs_rb.at[n], rs_r1.at[n], rs_r2.at[n],
            y, core, y_plus, y_minus, other,
        )

    def weight_gather(buf, half, low):
        rest = buf.shape[3] - half
        rows = buf.shape[2]
        a, b = pl.ds(0, half), pl.ds(half, rest)

        def rows_of(part):
            return pl.ds(0, rows) if part is None else (pl.ds(0, low), pl.ds(low, rows - low))[part]

        def pair(part):
            return pl.ds(0, 4) if part is None else pl.ds(2 * part, 2)

        return (
            RingGather(link, lambda i, p: buf.at[z, i, rows_of(p), a], x, x_plus, x_minus),
            RingGather(link, lambda i, p: buf.at[i, x, rows_of(p), b], z, z_plus, z_minus),
            RingGather(link, lambda i, p: buf.at[i, pair(p), :, a], z, z_plus, z_minus),
            RingGather(link, lambda i, p: buf.at[pair(p), i, :, b], x, x_plus, x_minus),
        )

    def weight_scatter(buf, half, low, a1, a2, b1, b2, a3, a4, b3, b4):
        rest = buf.shape[3] - half
        rows = buf.shape[2]
        a, b = pl.ds(0, half), pl.ds(half, rest)

        def rows_of(part):
            return pl.ds(0, rows) if part is None else (pl.ds(0, low), pl.ds(low, rows - low))[part]

        def pair(part):
            return pl.ds(0, 4) if part is None else pl.ds(2 * part, 2)

        cut = (pl.ds(0, low), pl.ds(low, rows - low))
        return (
            RingScatter(link, lambda i, p: buf.at[i, pair(p), :, a], z, z_plus, z_minus,
                        a1.at[0], a1.at[1], a2.at[0], a2.at[1]),
            RingScatter(link, lambda i, p: buf.at[pair(p), i, :, b], x, x_plus, x_minus,
                        b1.at[0], b1.at[1], b2.at[0], b2.at[1]),
            RingScatter(link, lambda i, p: buf.at[z, i, rows_of(p), a], x, x_plus, x_minus,
                        a3.at[cut[0]], a3.at[cut[1]], a4.at[0], a4.at[1]),
            RingScatter(link, lambda i, p: buf.at[i, x, rows_of(p), b], z, z_plus, z_minus,
                        b3.at[cut[0]], b3.at[cut[1]], b4.at[0], b4.at[1]),
        )

    xg[y, core] = x_ref[...]
    gather_x = ctx_gather(xg)
    pre_in[c] = win_ref[c]
    pre = []
    for step, mate in enumerate(mates):
        pre.append(
            (
                link.send(win_ref.at[mate[1]], pre_in.at[c], mate),
                link.send(pack_ref, pre_pack.at[step], mate),
            )
        )
    gather_x.start()
    wf[z, x] = wff_ref[...]
    cotg[y, core] = cot_ref[...]
    for step, (h_in, h_pack) in enumerate(pre):
        link.landed(h_in, pre_in.at[lax.rem(c + 7 - step, 8)])
        link.landed(h_pack, pre_pack.at[step])
    wc[z, x, 0:64, 0:384] = pre_in[...].reshape(64, 384).astype(bf16)
    wc[z, x, 0:64, 384:512] = wout_ref[...]
    own_pack = pack_ref[...]
    summed = own_pack
    for step in range(7):
        summed = summed + pre_pack[step]
    row = lax.broadcasted_iota(jnp.int32, (8, 128), 0)
    tile = jnp.where(row < 2, summed, own_pack)
    wc[z, x, 64:80, 0:128] = jnp.concatenate([tile, jnp.zeros_like(tile)], 0).astype(bf16)
    wc[z, x, 64:80, 128:512] = jnp.zeros((16, 384), bf16)
    conv_w = weight_gather(wc, 256, 48)
    ffn_w = weight_gather(wf, 896, 32)
    conv_w[0].start()
    conv_w[1].start()
    ffn_w[0].start()
    ffn_w[1].start()
    gather_x.forward()
    conv_w[0].forward()
    conv_w[1].forward()
    conv_w[0].finish()
    conv_w[1].finish()
    conv_w[2].start()
    conv_w[3].start()
    gather_x.across()
    ffn_w[0].forward()
    ffn_w[1].forward()
    conv_w[2].forward()
    conv_w[3].forward()
    ffn_w[0].finish()
    ffn_w[1].finish()
    ffn_w[2].start()
    ffn_w[3].start()
    gather_x.finish()
    gather_cot = ctx_gather(cotg)
    gather_cot.start()
    conv_w[2].finish()
    conv_w[3].finish()

    packs = [wc[i // 4, i % 4, 64:80, 0:128].astype(f32)[0:8] for i in range(16)]
    gain_one = jnp.concatenate([packs[2 * w][0:1] + packs[2 * w + 1][0:1] for w in range(8)], 1)
    gain_two = jnp.concatenate([packs[2 * w][1:2] + packs[2 * w + 1][1:2] for w in range(8)], 1)
    taps = packs[0]
    for i in range(1, 16):
        taps = taps + packs[i]
    tap = [taps[2 + k : 3 + k] for k in range(3)]
    w_in[...] = wc[:, :, 0:64, 0:384].reshape(1024, 384)
    slab = wc[:, :, 0:64, 384:512].astype(f32).reshape(16, 8, 8, 128)
    for w in range(8):
        w_out[:, 128 * w : 128 * w + 128] = slab[:, w].reshape(128, 128).astype(bf16)

    def project(g, carry):
        values = xg[g].reshape(256, 1024).astype(f32)
        scale = lax.rsqrt(jnp.mean(values * values, axis=-1, keepdims=True) + epsilon)
        scale_g[g] = scale
        lifted = (values * scale * gain_one).astype(bf16)
        h1g[g] = lifted
        proj[g] = mm(lifted, w_in[...])
        return carry

    lax.fori_loop(0, 4, project, 0)
    b_part = proj[:, :, 0:128].reshape(1024, 128)
    x_part = proj[:, :, 256:384].reshape(1024, 128)
    bx_pad[0:8] = jnp.zeros((8, 128), f32)
    bx_pad[8:1032] = (b_part * x_part).astype(bf16).astype(f32)
    z_all = tap[0] * bx_pad[6:1030] + tap[1] * bx_pad[7:1031] + tap[2] * bx_pad[8:1032]
    z_buf[...] = z_all
    y_buf[...] = (proj[:, :, 128:256].reshape(1024, 128) * z_all).astype(bf16).reshape(4, 256, 128)
    gather_cot.forward()
    ffn_w[2].forward()
    ffn_w[3].forward()

    scatter_r1 = ctx_scatter(0)

    def branch_out(step, carry):
        g = scatter_r1.group(step)
        rs_part[0, g] = mm(y_buf[g], w_out[...]).astype(bf16).reshape(2, 128, 1024)
        scatter_r1.cross(step)
        return carry

    lax.fori_loop(0, 4, branch_out, 0)
    scatter_r1.start()
    scatter_r1.middle()
    gather_cot.across()
    middle = x_ref[...].astype(f32) + scatter_r1.finish()
    scale_two = lax.rsqrt(jnp.mean(middle * middle, axis=-1, keepdims=True) + epsilon)
    h2g[y, core] = (middle * scale_two * gain_two).astype(bf16)
    gather_h2 = ctx_gather(h2g)
    gather_h2.start()
    gather_cot.finish()
    ffn_w[2].finish()
    ffn_w[3].finish()
    gather_h2.forward()
    gather_h2.across()
    gather_h2.finish()

    scatter_dh2 = ctx_scatter(1)
    low_half = lax.broadcasted_iota(jnp.int32, (256, 128), 1) < 64

    def feed_forward(step, carry):
        g = scatter_dh2.group(step)
        w_gu = wf[:, :, :, 0:GU].reshape(1024, GU)
        gu = mm(h2g[g].reshape(256, 1024), w_gu)
        mixed = gu[:, 1024:1152]
        gating = jnp.concatenate([gu[:, 0:512], mixed], 1)
        upward = jnp.concatenate([gu[:, 512:1024], pltpu.roll(mixed, 64, 1)], 1)
        sigma = 1.0 / (1.0 + jnp.exp(-gating))
        activated = gating * sigma
        hidden = activated * upward
        hid_buf[g, :, 0:512] = hidden[:, 0:512].astype(bf16)
        hid_buf[g, :, 512:640] = jnp.where(low_half, hidden[:, 512:640], 0.0).astype(bf16)
        w_down = wf[:, :, :, GU:FFL].reshape(1024, HID)
        d_hidden = mm(cotg[g].reshape(256, 1024), w_down)
        d_gating = d_hidden * upward * sigma * (1.0 + gating * (1.0 - sigma))
        d_upward = d_hidden * activated
        d_mixed = jnp.where(low_half, d_gating[:, 512:640], pltpu.roll(d_upward[:, 512:640], 64, 1))
        d_gu = jnp.concatenate([d_gating[:, 0:512], d_upward[:, 0:512], d_mixed], 1).astype(bf16)
        dgu_buf[g] = d_gu
        rs_part[1, g] = mt(d_gu, w_gu).astype(bf16).reshape(2, 128, 1024)
        scatter_dh2.cross(step)
        return carry

    lax.fori_loop(0, 4, feed_forward, 0)
    scatter_dh2.start()

    scatter_out = ctx_scatter(2)

    def ffn_out(step, carry):
        g = scatter_out.group(step)
        w_down = wf[:, :, :, GU:FFL].reshape(1024, HID)
        rs_part[2, g] = mt(hid_buf[g], w_down).astype(bf16).reshape(2, 128, 1024)
        scatter_out.cross(step)
        return carry

    lax.fori_loop(0, 4, ffn_out, 0)
    scatter_dh2.middle()

    def grad_gu(i, carry):
        lanes = pl.ds(pl.multiple_of(i * 256, 256), 256)
        lhs = h2g[:, :, :, lanes].reshape(1024, 256)
        gf[i, :, :, 0:GU] = tm(lhs, dgu_buf[...].reshape(1024, GU)).astype(bf16).reshape(4, 64, GU)
        return carry

    lax.fori_loop(0, 2, grad_gu, 0)

    d_second = scatter_dh2.finish()
    normed_two = middle * scale_two
    grad_gain_two = jnp.sum(d_second * normed_two, axis=0, keepdims=True)
    scaled = d_second * gain_two
    d_middle = cot_ref[...].astype(f32) + scale_two * (
        scaled - normed_two * jnp.mean(scaled * normed_two, axis=-1, keepdims=True)
    )
    dg[y, core] = d_middle.astype(bf16)
    gather_d = ctx_gather(dg)
    gather_d.start()

    lax.fori_loop(2, 4, grad_gu, 0)
    gather_d.forward()

    def grad_down(i, carry):
        lanes = pl.ds(pl.multiple_of(i * 256, 256), 256)
        lhs = cotg[:, :, :, lanes].reshape(1024, 256)
        gf[i, :, :, GU:FFL] = (
            tm(lhs, hid_buf[...].reshape(1024, HID)).astype(bf16).reshape(4, 64, HID)
        )
        return carry

    lax.fori_loop(0, 4, grad_down, 0)
    ffn_g = weight_scatter(gf, 896, 32, gf_a1, gf_a2, gf_b1, gf_b2, gf_a3, gf_a4, gf_b3, gf_b4)
    ffn_g[0].start()
    ffn_g[1].start()
    gather_d.across()
    scatter_out.start()
    gather_d.finish()

    d_z, d_c = [], []
    for g in range(4):
        d_gated = mt(dg[g].reshape(256, 1024), w_out[...])
        dz_pad[256 * g : 256 * g + 256] = d_gated * proj[g, :, 128:256]
        dp_buf[g, :, 128:256] = (d_gated * z_buf[256 * g : 256 * g + 256]).astype(bf16)
    dz_pad[1024:1032] = jnp.zeros((8, 128), f32)
    d_bx = tap[2] * dz_pad[0:1024] + tap[1] * dz_pad[1:1025] + tap[0] * dz_pad[2:1026]
    d_bx = d_bx.reshape(4, 256, 128)
    dp_buf[:, :, 0:128] = (d_bx * proj[:, :, 256:384]).astype(bf16)
    dp_buf[:, :, 256:384] = (d_bx * proj[:, :, 0:128]).astype(bf16)
    grad_tap = [
        jnp.sum(dz_pad[0:1024] * bx_pad[6 + k : 1030 + k], axis=0, keepdims=True) for k in range(3)
    ]
    ffn_g[0].middle()
    ffn_g[1].middle()

    scatter_dh1 = ctx_scatter(3)
    mix_acc[...] = jnp.zeros((8, 1024), f32)

    def branch_back(step, carry):
        g = scatter_dh1.group(step)
        d_lifted = mt(dp_buf[g], w_in[...])
        rs_part[3, g] = d_lifted.astype(bf16).reshape(2, 128, 1024)
        scatter_dh1.cross(step)
        normed = xg[g].reshape(256, 1024).astype(f32) * scale_g[g]
        mix_acc[...] += jnp.sum((d_lifted * normed).reshape(32, 8, 1024), axis=0)
        return carry

    lax.fori_loop(0, 4, branch_back, 0)
    scatter_dh1.start()

    def grad_in(i, carry):
        lanes = pl.ds(pl.multiple_of(i * 256, 256), 256)
        lhs = h1g[:, :, lanes].reshape(1024, 256)
        gc[i, :, 0:64, 0:384] = (
            tm(lhs, dp_buf[...].reshape(1024, 384)).astype(bf16).reshape(4, 64, 384)
        )
        return carry

    lax.fori_loop(0, 4, grad_in, 0)
    grad_mix = jnp.sum(mix_acc[...], axis=0, keepdims=True)
    g_out = tm(y_buf[...].reshape(1024, 128), dg[...].reshape(1024, 1024))
    pieces = [g_out[:, 128 * w : 128 * w + 128].reshape(16, 1, 8, 128) for w in range(8)]
    g_slab = jnp.concatenate(pieces, 1).reshape(4, 4, 64, 128)
    gc[:, :, 0:64, 384:512] = g_slab.astype(bf16)
    gc[:, :, 64:80, 128:512] = jnp.zeros((4, 4, 16, 384), bf16)
    for i in range(16):
        lanes = slice(128 * (i // 2), 128 * (i // 2) + 128)
        rows = [grad_mix[:, lanes], grad_gain_two[:, lanes], *grad_tap, jnp.zeros((11, 128), f32)]
        gc[i // 4, i % 4, 64:80, 0:128] = jnp.concatenate(rows, 0).astype(bf16)
    conv_g = weight_scatter(gc, 256, 48, gc_a1, gc_a2, gc_b1, gc_b2, gc_a3, gc_a4, gc_b3, gc_b4)
    conv_g[0].start()
    conv_g[1].start()
    scatter_dh1.middle()
    ffn_g[0].finish()
    ffn_g[1].finish()
    ffn_g[2].start()
    ffn_g[3].start()
    conv_g[0].middle()
    conv_g[1].middle()
    scatter_out.middle()

    d_lifted = scatter_dh1.finish()
    local = x_ref[...].astype(f32)
    scale_one = lax.rsqrt(jnp.mean(local * local, axis=-1, keepdims=True) + epsilon)
    normed_one = local * scale_one
    scaled = d_lifted * gain_one
    gin_ref[...] = d_middle + scale_one * (
        scaled - normed_one * jnp.mean(scaled * normed_one, axis=-1, keepdims=True)
    )
    conv_g[0].finish()
    conv_g[1].finish()
    conv_g[2].start()
    conv_g[3].start()
    ffn_g[2].middle()
    ffn_g[3].middle()
    conv_g[2].middle()
    conv_g[3].middle()
    out_ref[...] = (middle + scatter_out.finish()).astype(bf16)
    conv_g[2].finish()
    conv_g[3].finish()

    total = gc[z, x].astype(f32)
    gwout_ref[...] = total[0:64, 384:512]
    post_send[...] = total[0:64, 0:384].reshape(8, 8, 384)
    post_own[...] = total[64:72, 0:128]
    post = []
    for step, mate in enumerate(mates):
        post.append(
            (
                link.send(post_send.at[mate[1]], post_in.at[c], mate),
                link.send(post_own, post_pack.at[step], mate),
            )
        )
    ffn_g[2].finish()
    ffn_g[3].finish()
    gff_ref[...] = gf[z, x].astype(f32)
    post_in[c] = post_send[c]
    summed = post_own[...]
    for step, (h_in, h_pack) in enumerate(post):
        link.landed(h_in, post_in.at[lax.rem(c + 7 - step, 8)])
        link.landed(h_pack, post_pack.at[step])
        summed = summed + post_pack[step]
    gwin_ref[...] = post_in[...]
    gpack_ref[...] = jnp.where(row < 2, summed, post_own[...])

    link.drain()
    for scatter in (scatter_r1, scatter_dh2, scatter_out, scatter_dh1):
        scatter.drain()


def per_device(
    inputs,
    mix_gain,
    in_proj,
    conv_kernel,
    out_proj,
    ffn_gain,
    gate_proj,
    up_proj,
    down_proj,
    cotangent,
):
    f = lax.axis_index("fsdp")
    c = lax.axis_index("ctx")
    wff = jnp.concatenate(
        [
            gate_proj[:, :512],
            up_proj[:, :512],
            gate_proj[:, 512:],
            up_proj[:, 512:],
            down_proj.T,
            jnp.zeros((64, 64), bf16),
        ],
        1,
    )
    win = in_proj.reshape(8, 3, 16, 8, 8).transpose(3, 0, 1, 2, 4).reshape(8, 8, 384).astype(f32)
    wout = out_proj.reshape(8, 8, 128).transpose(1, 0, 2).reshape(64, 128)
    gains = jnp.stack([mix_gain, ffn_gain], 0).astype(f32)
    pack = jnp.zeros((8, 128), f32)
    pack = lax.dynamic_update_slice(pack, gains, (0, 64 * (f % 2) + 8 * c))
    pack = lax.dynamic_update_slice(pack, conv_kernel.astype(f32), (2, 8 * f))

    v = pltpu.VMEM
    in_vmem = pl.BlockSpec(memory_space=pltpu.VMEM)
    sems = 192
    out_shape = (
        jax.ShapeDtypeStruct((128, 1024), bf16),
        jax.ShapeDtypeStruct((128, 1024), f32),
        jax.ShapeDtypeStruct((64, FFL), f32),
        jax.ShapeDtypeStruct((8, 8, 384), f32),
        jax.ShapeDtypeStruct((64, 128), f32),
        jax.ShapeDtypeStruct((8, 128), f32),
    )
    scratch = [
        pltpu.SemaphoreType.DMA((sems,)),
        pltpu.SemaphoreType.DMA((sems,)),
        v((4, 2, 128, 1024), bf16),
        v((4, 2, 128, 1024), bf16),
        v((4, 2, 128, 1024), bf16),
        v((4, 2, 128, 1024), bf16),
        v((4, 4, 64, FFL), bf16),
        v((4, 4, CR, CL), bf16),
        v((8, 8, 384), f32),
        v((7, 8, 128), f32),
        v((1024, 384), bf16),
        v((128, 1024), bf16),
        v((4, 256, 1024), bf16),
        v((4, 256, 1), f32),
        v((4, 256, 384), f32),
        v((1032, 128), f32),
        v((1024, 128), f32),
        v((4, 256, 128), bf16),
        v((4, 256, HID), bf16),
        v((4, 256, GU), bf16),
        v((1032, 128), f32),
        v((4, 256, 384), bf16),
        v((8, 1024), f32),
        v((4, 4, 2, 128, 1024), bf16),
        v((4, 4, 128, 1024), bf16),
        v((4, 2, 64, 1024), bf16),
        v((4, 2, 128, 1024), bf16),
        v((4, 4, 64, FFL), bf16),
        v((4, 4, CR, CL), bf16),
        v((2, 2, 64, 896), bf16),
        v((2, 4, 64, 896), bf16),
        v((2, 2, 64, 896), bf16),
        v((2, 4, 64, 896), bf16),
        v((64, 896), bf16),
        v((2, 64, 896), bf16),
        v((64, 896), bf16),
        v((2, 64, 896), bf16),
        v((2, 2, CR, 256), bf16),
        v((2, 4, CR, 256), bf16),
        v((2, 2, CR, 256), bf16),
        v((2, 4, CR, 256), bf16),
        v((CR, 256), bf16),
        v((2, CR, 256), bf16),
        v((CR, 256), bf16),
        v((2, CR, 256), bf16),
        v((8, 8, 384), f32),
        v((8, 8, 384), f32),
        v((8, 128), f32),
        v((7, 8, 128), f32),
    ]
    block_out, grad_inputs, gff, gwin, gwout, gpack = pl.pallas_call(
        block_kernel,
        out_shape=out_shape,
        in_specs=[in_vmem] * 6,
        out_specs=(in_vmem,) * 6,
        scratch_shapes=scratch,
        compiler_params=pltpu.CompilerParams(
            collective_id=0, has_side_effects=True, vmem_limit_bytes=62 * 1024 * 1024
        ),
    )(inputs.reshape(128, 1024), cotangent.reshape(128, 1024), wff, win, wout, pack)

    grad_gains = lax.dynamic_slice(gpack, (0, 64 * (f % 2) + 8 * c), (2, 8))
    grad_taps = lax.dynamic_slice(gpack, (2, 8 * f), (3, 8))
    grad_in = gwin.reshape(8, 8, 3, 16, 8).transpose(1, 2, 3, 0, 4).reshape(8, 3072)
    grad_out = gwout.reshape(8, 8, 128).transpose(1, 0, 2).reshape(8, 1024)
    return (
        block_out.reshape(inputs.shape),
        grad_inputs.reshape(inputs.shape),
        grad_gains[0],
        grad_in,
        grad_taps,
        grad_out,
        grad_gains[1],
        jnp.concatenate([gff[:, :512], gff[:, 1024:1088]], 1),
        jnp.concatenate([gff[:, 512:1024], gff[:, 1088:1152]], 1),
        gff[:, 1152:1728].T,
    )


def solution(mesh):
    in_specs = (
        P("fsdp", "ctx", None),
        P(("fsdp", "ctx")),
        P(("fsdp", "ctx"), None),
        P(None, ("fsdp", "ctx")),
        P(("fsdp", "ctx"), None),
        P(("fsdp", "ctx")),
        P("fsdp", "ctx"),
        P("fsdp", "ctx"),
        P("ctx", "fsdp"),
        P("fsdp", "ctx", None),
    )
    out_specs = (
        P("fsdp", "ctx", None),
        P("fsdp", "ctx", None),
        P(("fsdp", "ctx")),
        P(("fsdp", "ctx"), None),
        P(None, ("fsdp", "ctx")),
        P(("fsdp", "ctx"), None),
        P(("fsdp", "ctx")),
        P("fsdp", "ctx"),
        P("fsdp", "ctx"),
        P("ctx", "fsdp"),
    )
    return jax.shard_map(
        per_device, mesh=mesh, in_specs=in_specs, out_specs=out_specs, check_vma=False
    )
```

time: 1740 us -> 166 us (0.10)
  waiting for transfers between devices: 1440 us -> 0 us
  blocking collectives: 166 us -> 0 us
  Pallas kernels: 0 us -> 145 us
  matrix products: 81.6 us -> 0 us
    reduce_scatter x5 -> x0, waiting for transfers between devices: 1020 us -> none  [the longest x1 638 us: per_device(): lax.psum_scatter(grad_out, ('fsdp', 'ctx'), scatter_dimension=0, tiled=True)]
    all_gather x8 -> x0, waiting for transfers between devices: 304 us -> none  [the longest x1 50.9 us: per_device(): lax.all_gather(row_weights[0], 'ctx', axis=1, tiled=True)]
    pallas_call x0 -> x1, Pallas kernels: none -> 145 us  [per_device(): pl.pallas_call(block_kernel, out_shape=out_shape, in_specs=[in_vmem] * 6,...]
    unnamed x2 -> x0, blocking collectives: 132 us -> none
    unnamed x19 -> x0, waiting for transfers between devices: 116 us -> none
    dot_general x15 -> x0, matrix products: 81.6 us -> none  [the longest x1 10.1 us: ffn_backward(): d_hidden = jnp.dot(rows_cot, w_down.T, preferred_element_type=jnp.float32)]
    all_gather x1 -> x0, blocking collectives: 34.1 us -> none  [per_device(): lax.all_gather(conv_kernel, ('fsdp', 'ctx'), axis=1, tiled=True)]
  transfers between devices with their start and end apart: 18 -> 0, of which waited for: 16 -> 0; matrix products, arithmetic and copies ran while one was open for 5% -> 0% of each run, Pallas kernels for 0% -> 0%
where the time goes in v1:
time: 166 us; the launch traced here: 165 us
  Pallas kernels  145 us (87%)
  local copies, waits for them, and re-layouts  18.5 us (11%)
    pallas_call x1, Pallas kernels, per_device(): pl.pallas_call(block_kernel, out_shape=out_shape, in_specs=[in_vmem] * 6,...  145 us
    convert_element_type x3, local copies, waits for them, and re-layouts, per_device(): in_proj.reshape(8, 3, 16, 8, 8).transpose(3, 0, 1, 2, 4).reshape(8, 8, 384)  3.33 us

profile of v1, /device:TPU:1, one launch (start us, length us, event | category | flops | bytes accessed | tf_op | source)
XLA Modules:
  0.0 165.1 jit_solution(8563371366006827695)
XLA Ops:
  0.6 0.8 slice.33
  1.5 0.8 slice.34
  2.3 0.7 slice.35
  3.1 0.7 slice.36
  3.8 1.7 %concatenate.9.wff_ref = bf16[64,1792]{1,0:T(8,128)(2,1)} concatenate(bf16[64,512]{1,0:T(8,128)(2,1)S(1)} %slice.33, bf16[64,512]{1,0:T(8,128)(2,1)S(1)} %slice.34, bf16[64,64]{1,0:T(8,128)(2,1)S(1)} %slice.35, bf16[64,64]{1,0:T(8,128)(2,1)S(1)} %slice.36, bf16[64,576]{1,0:T(8,128)(2,1)} %bitcast.35, bf16[64,64]{1,0:T(8,128)(2,1)S(1)} %broadcast_in_dim.6), dimensions={1} | concatenate | bytes 458752 | tf_op jit(solution)/shard_map/concatenate | solution.py:672
  5.4 1.7 %reshape.67 = f32[8,3,16,8,8]{4,3,2,1,0:T(8,128)S(1)} reshape(bf16[8,3072]{1,0:T(8,128)(2,1)} %param.12) | data formatting | bytes 147456 | tf_op jit(solution)/shard_map/convert_element_type | solution.py:683
  7.1 0.3 copy.22
  7.5 1.4 reshape.66.win_ref
  8.9 0.5 dynamic_update_slice.6
  9.4 0.3 dynamic_update_slice.7.pack_ref
  9.7 0.6 copy-done.4
  10.3 145.1 %shard_map.177 = (bf16[128,1024]{1,0:T(8,128)(2,1)}, f32[128,1024]{1,0:T(8,128)}, f32[64,1792]{1,0:T(8,128)}, f32[8,8,384]{2,1,0:T(8,128)}, f32[64,128]{1,0:T(8,128)}, /*index=5*/f32[8,128]{1,0:T(8,128)}) custom-call(bf16[128,1024]{1,0:T(8,128)(2,1)} %bitcast.32, bf16[128,1024]{1,0:T(8,128)(2,1)} %bitcast.33, bf16[64,1792]{1,0:T(8,128)(2,1)} %concatenate.9.wff_ref, ...), custom_call_target="tpu_custom_call" | custom-call | tf_op jit(solution)/shard_map/pallas_call | solution.py:752
  155.4 0.7 constant_dynamic-slice_fusion.1
  156.1 0.5 slice_bitcast_fusion.1
  156.7 1.7 %reshape.62 = f32[8,8,3,16,8]{4,3,2,1,0:T(8,128)S(1)} reshape(f32[8,8,384]{2,1,0:T(8,128)} %get-tuple-element.19) | data formatting | bytes 196608 | tf_op jit(solution)/shard_map/reshape | solution.py:765
  158.4 0.9 copy.23
  159.4 1.5 reshape.63
  160.8 0.6 constant_dynamic-slice_fusion
  161.5 0.1 fusion.1
  161.6 0.7 pad_maximum_fusion
  162.3 0.7 slice_bitcast_fusion
  163.0 0.7 copy.29
  163.7 0.8 copy.30
  164.5 0.6 copy.31
  (22 shorter events, 0.1 us)
Async XLA Ops:
  7.4 1.4 copy-start.7
  7.4 1.4 copy-start.8
  7.5 1.9 %copy-start.6 = (bf16[3,8]{1,0:T(4,128)(2,1)S(1)}, bf16[3,8]{1,0:T(4,128)(2,1)}, u32[]{:S(2)}) copy-start(bf16[3,8]{1,0:T(4,128)(2,1)} %param.13) | copy-start | bytes 148
  9.7 0.6 copy-start.4
  159.3 1.5 copy-start.5
  159.3 2.2 %copy-start = (f32[64,1792]{1,0:T(8,128)S(1)}, f32[64,1792]{1,0:T(8,128)}, u32[]{:S(2)}) copy-start(f32[64,1792]{1,0:T(8,128)} %get-tuple-element.21) | copy-start | bytes 1376260
  159.3 3.7 %copy-start.2 = (bf16[128,1024]{1,0:T(8,128)(2,1)S(1)}, bf16[128,1024]{1,0:T(8,128)(2,1)}, u32[]{:S(2)}) copy-start(bf16[128,1024]{1,0:T(8,128)(2,1)} %get-tuple-element.16) | copy-start | bytes 786436
  159.4 4.4 %copy-start.1 = (f32[128,1024]{1,0:T(8,128)S(1)}, f32[128,1024]{1,0:T(8,128)}, u32[]{:S(2)}) copy-start(f32[128,1024]{1,0:T(8,128)} %get-tuple-element.17) | copy-start | bytes 1572868
  161.6 3.0 %copy-start.3 = (f32[64,128]{1,0:T(8,128)S(1)}, f32[64,128]{1,0:T(8,128)}, u32[]{:S(2)}) copy-start(f32[64,128]{1,0:T(8,128)} %get-tuple-element.20) | copy-start | bytes 98308

commit v2 on v1

--- a/solution.py
+++ b/solution.py
@@ -125,41 +125,83 @@
         add_into(self.view(self.me, None), self.r2a, self.r2b)
 
 
+class DirectGather:
+    def __init__(self, link, view, me, device):
+        self.link, self.view, self.me, self.device = link, view, me, device
+
+    def start(self):
+        own = self.view(self.me, None)
+        self.sent = [(s, self.link.send(own, own, self.device(s))) for s in (1, 3, 2)]
+
+    def finish(self):
+        for step, handle in self.sent:
+            self.link.landed(handle, self.view(ring(self.me, 4 - step), None))
+
+
+class DirectScatter:
+    def __init__(self, link, view, me, device, landing):
+        self.link, self.view, self.me, self.device, self.landing = link, view, me, device, landing
+
+    def start(self):
+        self.sent = [
+            (s, self.link.send(self.view(ring(self.me, s), None), self.landing.at[s - 1], self.device(s)))
+            for s in (1, 3, 2)
+        ]
+
+    def finish(self):
+        for step, handle in self.sent:
+            self.link.landed(handle, self.landing.at[step - 1])
+        add_into(self.view(self.me, None), *[self.landing.at[i] for i in range(3)])
+
+
+LO, HI = pl.ds(0, 64), pl.ds(64, 64)
+
+
 class CtxGather:
     def __init__(self, link, buf, y, core, plus, minus, other):
         self.link, self.buf, self.y, self.core = link, buf, y, core
         self.plus, self.minus, self.other = plus, minus, other
 
     def half(self, which, part):
-        return self.buf.at[which, self.core, pl.ds(64 * part, 64)]
+        return self.buf.at[which, self.core, (LO, HI)[part]]
 
     def start(self):
+        send = self.link.send
+        lo, hi = self.half(self.y, 0), self.half(self.y, 1)
         own = self.buf.at[self.y, self.core]
-        self.hp = self.link.send(own, own, self.plus)
-        self.hm = self.link.send(own, own, self.minus)
-        self.ho = [self.link.send(own, own, self.other)]
+        self.p0, self.m1 = send(lo, lo, self.plus), send(hi, hi, self.minus)
+        self.p1, self.m0 = send(hi, hi, self.plus), send(lo, lo, self.minus)
+        self.near = send(own, own, self.other)
+        self.late = []
+
+    def pass_on(self, handle, which, part, device):
+        half = self.half(which, part)
+        self.link.landed(handle, half)
+        onward = None if device is None else self.link.send(half, half, device)
+        theirs = self.buf.at[which, 1 - self.core, (LO, HI)[part]]
+        self.late.append((self.link.send(half, half, self.other), theirs))
+        return onward
 
     def forward(self):
         left, right = ring(self.y, 3), ring(self.y, 1)
-        block = self.buf.at[left, self.core]
-        self.link.landed(self.hp, block)
-        self.fp = self.link.send(self.half(left, 0), self.half(left, 0), self.plus)
-        self.ho.append(self.link.send(block, block, self.other))
-        block = self.buf.at[right, self.core]
-        self.link.landed(self.hm, block)
-        self.fm = self.link.send(self.half(right, 1), self.half(right, 1), self.minus)
-        self.ho.append(self.link.send(block, block, self.other))
+        self.fp = self.pass_on(self.p0, left, 0, self.plus)
+        self.fm = self.pass_on(self.m1, right, 1, self.minus)
+
+    def sides(self):
+        self.pass_on(self.p1, ring(self.y, 3), 1, None)
+        self.pass_on(self.m0, ring(self.y, 1), 0, None)
 
     def across(self):
         far = ring(self.y, 2)
-        self.link.landed(self.fp, self.half(far, 0))
-        self.link.landed(self.fm, self.half(far, 1))
-        block = self.buf.at[far, self.core]
-        self.ho.append(self.link.send(block, block, self.other))
-
-    def finish(self):
-        for handle, step in zip(self.ho, (0, 3, 1, 2)):
-            self.link.landed(handle, self.buf.at[ring(self.y, step), 1 - self.core])
+        self.pass_on(self.fp, far, 0, None)
+        self.pass_on(self.fm, far, 1, None)
+
+    def finish_near(self):
+        self.link.landed(self.near, self.buf.at[self.y, 1 - self.core])
+
+    def finish_far(self):
+        for handle, ref in self.late:
+            self.link.landed(handle, ref)
 
 
 class CtxScatter:
@@ -182,33 +224,41 @@
         ref = self.rb.at[g]
         self.link.copy(ref, ref, self.other, self.first + step).wait_recv()
 
+    def block(self, which, rows):
+        return self.part.at[which, self.core, rows]
+
     def start(self):
         far = ring(self.y, 2)
         self.crossed(far, 0)
-        block = self.part.at[far, self.core]
-        add_into(block, self.rb.at[far])
-        self.h1a = self.link.send(block.at[pl.ds(0, 64)], self.r1.at[0], self.plus)
-        self.h1b = self.link.send(block.at[pl.ds(64, 64)], self.r1.at[1], self.minus)
+        add_into(self.block(far, LO), self.rb.at[far, LO])
+        self.h1a = self.link.send(self.block(far, LO), self.r1.at[0], self.plus)
+        add_into(self.block(far, HI), self.rb.at[far, HI])
+        self.h1b = self.link.send(self.block(far, HI), self.r1.at[1], self.minus)
+
+    def sides(self):
+        left, right = ring(self.y, 3), ring(self.y, 1)
+        self.crossed(left, 1)
+        add_into(self.block(left, LO), self.rb.at[left, LO])
+        self.h2b0 = self.link.send(self.block(left, LO), self.r2.at[1, LO], self.minus)
+        self.crossed(right, 2)
+        add_into(self.block(right, HI), self.rb.at[right, HI])
+        self.h2a1 = self.link.send(self.block(right, HI), self.r2.at[0, HI], self.plus)
 
     def middle(self):
         left, right = ring(self.y, 3), ring(self.y, 1)
-        self.crossed(left, 1)
-        self.crossed(right, 2)
-        block = self.part.at[right, self.core]
         self.link.landed(self.h1a, self.r1.at[0])
-        add_into(block.at[pl.ds(0, 64)], self.rb.at[right, pl.ds(0, 64)], self.r1.at[0])
-        add_into(block.at[pl.ds(64, 64)], self.rb.at[right, pl.ds(64, 64)])
-        self.h2a = self.link.send(block, self.r2.at[0], self.plus)
-        block = self.part.at[left, self.core]
+        add_into(self.block(right, LO), self.rb.at[right, LO], self.r1.at[0])
+        self.h2a0 = self.link.send(self.block(right, LO), self.r2.at[0, LO], self.plus)
         self.link.landed(self.h1b, self.r1.at[1])
-        add_into(block.at[pl.ds(0, 64)], self.rb.at[left, pl.ds(0, 64)])
-        add_into(block.at[pl.ds(64, 64)], self.rb.at[left, pl.ds(64, 64)], self.r1.at[1])
-        self.h2b = self.link.send(block, self.r2.at[1], self.minus)
+        add_into(self.block(left, HI), self.rb.at[left, HI], self.r1.at[1])
+        self.h2b1 = self.link.send(self.block(left, HI), self.r2.at[1, HI], self.minus)
 
     def finish(self):
         self.crossed(self.y, 3)
-        self.link.landed(self.h2a, self.r2.at[0])
-        self.link.landed(self.h2b, self.r2.at[1])
+        self.link.landed(self.h2b0, self.r2.at[1, LO])
+        self.link.landed(self.h2a1, self.r2.at[0, HI])
+        self.link.landed(self.h2a0, self.r2.at[0, LO])
+        self.link.landed(self.h2b1, self.r2.at[1, HI])
         return (
             self.part[self.y, self.core].astype(f32)
             + self.rb[self.y].astype(f32)
@@ -223,13 +273,33 @@
             self.link.copy(src, src, self.other, self.first + step).wait_send()
 
 
+def by_channel(blocks, lane, inverse):
+    made = []
+    for target in range(8):
+        total = jnp.zeros((8, 128), f32)
+        for source in range(8):
+            for h in range(2):
+                if inverse:
+                    start, lands = 16 * target + 8 * h, 64 * h + 8 * source
+                else:
+                    start, lands = 64 * h + 8 * target, 16 * source + 8 * h
+                moved = pltpu.roll(blocks[source], (lands - start) % 128, 1)
+                total = jnp.where((lane >= lands) & (lane < lands + 8), moved, total)
+        made.append(total)
+    return made
+
+
 def block_kernel(
     x_ref,
     cot_ref,
-    wff_ref,
-    win_ref,
-    wout_ref,
-    pack_ref,
+    mix_ref,
+    in_ref,
+    tap_ref,
+    proj_ref,
+    ffn_ref,
+    gate_ref,
+    up_ref,
+    down_ref,
     out_ref,
     gin_ref,
     gff_ref,
@@ -238,6 +308,8 @@
     gpack_ref,
     send_sems,
     recv_sems,
+    win_ref,
+    pack_ref,
     xg,
     cotg,
     h2g,
@@ -273,14 +345,8 @@
     gf_a4,
     gf_b3,
     gf_b4,
-    gc_a1,
-    gc_a2,
-    gc_b1,
-    gc_b2,
-    gc_a3,
-    gc_a4,
-    gc_b3,
-    gc_b4,
+    gc_r1,
+    gc_r2,
     post_send,
     post_in,
     post_own,
@@ -294,12 +360,38 @@
     other = (f, y * 2 + 1 - core)
     x_plus, x_minus = (z * 4 + ring(x, 1), c), (z * 4 + ring(x, 3), c)
     z_plus, z_minus = (ring(z, 1) * 4 + x, c), (ring(z, 3) * 4 + x, c)
+
+    def along_x(step):
+        return (z * 4 + ring(x, step), c)
+
+    def along_z(step):
+        return (ring(z, step) * 4 + x, c)
+
     mates = [(f, lax.rem(c + step, 8)) for step in range(1, 8)]
 
     barrier = pltpu.get_barrier_semaphore()
-    for device in mates + [x_plus, x_minus, z_plus, z_minus]:
+    rings = [along_x(step) for step in (1, 2, 3)] + [along_z(step) for step in (1, 2, 3)]
+    for device in mates + rings:
         pl.semaphore_signal(barrier, inc=1, device_id=device, device_id_type=MESH)
-    pl.semaphore_wait(barrier, 11)
+
+    lane = lax.broadcasted_iota(jnp.int32, (8, 128), 1)
+    row = lax.broadcasted_iota(jnp.int32, (8, 128), 0)
+    xg[y, core] = x_ref[0]
+    in_rows = in_ref[...].astype(f32)
+    for b in range(3):
+        blocks = [in_rows[:, 1024 * b + 128 * v : 1024 * b + 128 * v + 128] for v in range(8)]
+        for channel, block in enumerate(by_channel(blocks, lane, False)):
+            win_ref[channel, :, 128 * b : 128 * b + 128] = block
+    pack_ref[...] = jnp.zeros((8, 128), f32)
+    pack_ref[0:1, 0:8] = mix_ref[...].astype(f32)
+    pack_ref[1:2, 0:8] = ffn_ref[...].astype(f32)
+    pack_ref[2:5, 0:8] = tap_ref[...].astype(f32)
+    small = pack_ref[...]
+    gains = pltpu.roll(small, 64 * lax.rem(f, 2) + 8 * c, 1)
+    own_pack = jnp.where(row < 2, gains, pltpu.roll(small, 8 * f, 1))
+    pack_ref[...] = own_pack
+    pre_in[c] = win_ref[c]
+    pl.semaphore_wait(barrier, 13)
 
     link = Link(send_sems, recv_sems)
 
@@ -328,6 +420,24 @@
             RingGather(link, lambda i, p: buf.at[i, x, rows_of(p), b], z, z_plus, z_minus),
             RingGather(link, lambda i, p: buf.at[i, pair(p), :, a], z, z_plus, z_minus),
             RingGather(link, lambda i, p: buf.at[pair(p), i, :, b], x, x_plus, x_minus),
+        )
+
+    def conv_gather(buf):
+        a, b = pl.ds(0, 256), pl.ds(256, 256)
+        return (
+            DirectGather(link, lambda i, p: buf.at[z, i, :, a], x, along_x),
+            DirectGather(link, lambda i, p: buf.at[i, x, :, b], z, along_z),
+            DirectGather(link, lambda i, p: buf.at[i, :, :, a], z, along_z),
+            DirectGather(link, lambda i, p: buf.at[:, i, :, b], x, along_x),
+        )
+
+    def conv_scatter(buf, r1, r2):
+        a, b = pl.ds(0, 256), pl.ds(256, 256)
+        return (
+            DirectScatter(link, lambda i, p: buf.at[i, :, :, a], z, along_z, r1.at[0]),
+            DirectScatter(link, lambda i, p: buf.at[:, i, :, b], x, along_x, r1.at[1]),
+            DirectScatter(link, lambda i, p: buf.at[z, i, :, a], x, along_x, r2.at[0]),
+            DirectScatter(link, lambda i, p: buf.at[i, x, :, b], z, along_z, r2.at[1]),
         )
 
     def weight_scatter(buf, half, low, a1, a2, b1, b2, a3, a4, b3, b4):
@@ -353,9 +463,6 @@
                         b3.at[cut[0]], b3.at[cut[1]], b4.at[0], b4.at[1]),
         )
 
-    xg[y, core] = x_ref[...]
-    gather_x = ctx_gather(xg)
-    pre_in[c] = win_ref[c]
     pre = []
     for step, mate in enumerate(mates):
         pre.append(
@@ -364,31 +471,38 @@
                 link.send(pack_ref, pre_pack.at[step], mate),
             )
         )
+    gather_x = ctx_gather(xg)
     gather_x.start()
-    wf[z, x] = wff_ref[...]
-    cotg[y, core] = cot_ref[...]
+    own = wf.at[z, x]
+    own[:, 0:512] = gate_ref[:, 0:512]
+    own[:, 512:1024] = up_ref[:, 0:512]
+    own[:, 1024:1152] = jnp.concatenate([gate_ref[:, 512:576], up_ref[:, 512:576]], 1)
+    own[:, 1152:1792] = jnp.concatenate(
+        [down_ref[...].astype(f32).T, jnp.zeros((64, 64), f32)], 1
+    ).astype(bf16)
+    cotg[y, core] = cot_ref[0]
+    out_rows = proj_ref[...].astype(f32)
+    wc[z, x, 0:64, 384:512] = jnp.concatenate(
+        [out_rows[:, 128 * w : 128 * w + 128] for w in range(8)], 0
+    ).astype(bf16)
+    wc[z, x, 64:80, 128:512] = jnp.zeros((16, 384), bf16)
+    conv_w = conv_gather(wc)
+    ffn_w = weight_gather(wf, 896, 32)
     for step, (h_in, h_pack) in enumerate(pre):
         link.landed(h_in, pre_in.at[lax.rem(c + 7 - step, 8)])
         link.landed(h_pack, pre_pack.at[step])
     wc[z, x, 0:64, 0:384] = pre_in[...].reshape(64, 384).astype(bf16)
-    wc[z, x, 0:64, 384:512] = wout_ref[...]
-    own_pack = pack_ref[...]
     summed = own_pack
     for step in range(7):
         summed = summed + pre_pack[step]
-    row = lax.broadcasted_iota(jnp.int32, (8, 128), 0)
     tile = jnp.where(row < 2, summed, own_pack)
     wc[z, x, 64:80, 0:128] = jnp.concatenate([tile, jnp.zeros_like(tile)], 0).astype(bf16)
-    wc[z, x, 64:80, 128:512] = jnp.zeros((16, 384), bf16)
-    conv_w = weight_gather(wc, 256, 48)
-    ffn_w = weight_gather(wf, 896, 32)
     conv_w[0].start()
     conv_w[1].start()
+    gather_x.forward()
     ffn_w[0].start()
     ffn_w[1].start()
-    gather_x.forward()
-    conv_w[0].forward()
-    conv_w[1].forward()
+    gather_x.sides()
     conv_w[0].finish()
     conv_w[1].finish()
     conv_w[2].start()
@@ -396,17 +510,16 @@
     gather_x.across()
     ffn_w[0].forward()
     ffn_w[1].forward()
-    conv_w[2].forward()
-    conv_w[3].forward()
+    gather_x.finish_near()
+    gather_x.finish_far()
+    gather_cot = ctx_gather(cotg)
+    gather_cot.start()
+    conv_w[2].finish()
+    conv_w[3].finish()
     ffn_w[0].finish()
     ffn_w[1].finish()
     ffn_w[2].start()
     ffn_w[3].start()
-    gather_x.finish()
-    gather_cot = ctx_gather(cotg)
-    gather_cot.start()
-    conv_w[2].finish()
-    conv_w[3].finish()
 
     packs = [wc[i // 4, i % 4, 64:80, 0:128].astype(f32)[0:8] for i in range(16)]
     gain_one = jnp.concatenate([packs[2 * w][0:1] + packs[2 * w + 1][0:1] for w in range(8)], 1)
@@ -438,6 +551,7 @@
     z_buf[...] = z_all
     y_buf[...] = (proj[:, :, 128:256].reshape(1024, 128) * z_all).astype(bf16).reshape(4, 256, 128)
     gather_cot.forward()
+    gather_cot.sides()
     ffn_w[2].forward()
     ffn_w[3].forward()
 
@@ -451,19 +565,23 @@
 
     lax.fori_loop(0, 4, branch_out, 0)
     scatter_r1.start()
+    scatter_r1.sides()
     scatter_r1.middle()
     gather_cot.across()
-    middle = x_ref[...].astype(f32) + scatter_r1.finish()
+    middle = x_ref[0].astype(f32) + scatter_r1.finish()
     scale_two = lax.rsqrt(jnp.mean(middle * middle, axis=-1, keepdims=True) + epsilon)
     h2g[y, core] = (middle * scale_two * gain_two).astype(bf16)
     gather_h2 = ctx_gather(h2g)
     gather_h2.start()
-    gather_cot.finish()
+    gather_cot.finish_near()
+    gather_cot.finish_far()
     ffn_w[2].finish()
     ffn_w[3].finish()
     gather_h2.forward()
+    gather_h2.sides()
     gather_h2.across()
-    gather_h2.finish()
+    gather_h2.finish_near()
+    gather_h2.finish_far()
 
     scatter_dh2 = ctx_scatter(1)
     low_half = lax.broadcasted_iota(jnp.int32, (256, 128), 1) < 64
@@ -493,6 +611,7 @@
 
     lax.fori_loop(0, 4, feed_forward, 0)
     scatter_dh2.start()
+    scatter_dh2.sides()
 
     scatter_out = ctx_scatter(2)
 
@@ -518,7 +637,7 @@
     normed_two = middle * scale_two
     grad_gain_two = jnp.sum(d_second * normed_two, axis=0, keepdims=True)
     scaled = d_second * gain_two
-    d_middle = cot_ref[...].astype(f32) + scale_two * (
+    d_middle = cot_ref[0].astype(f32) + scale_two * (
         scaled - normed_two * jnp.mean(scaled * normed_two, axis=-1, keepdims=True)
     )
     dg[y, core] = d_middle.astype(bf16)
@@ -527,6 +646,7 @@
 
     lax.fori_loop(2, 4, grad_gu, 0)
     gather_d.forward()
+    gather_d.sides()
 
     def grad_down(i, carry):
         lanes = pl.ds(pl.multiple_of(i * 256, 256), 256)
@@ -542,9 +662,10 @@
     ffn_g[1].start()
     gather_d.across()
     scatter_out.start()
-    gather_d.finish()
-
-    d_z, d_c = [], []
+    scatter_out.sides()
+    gather_d.finish_near()
+    gather_d.finish_far()
+
     for g in range(4):
         d_gated = mt(dg[g].reshape(256, 1024), w_out[...])
         dz_pad[256 * g : 256 * g + 256] = d_gated * proj[g, :, 128:256]
@@ -574,6 +695,7 @@
 
     lax.fori_loop(0, 4, branch_back, 0)
     scatter_dh1.start()
+    scatter_dh1.sides()
 
     def grad_in(i, carry):
         lanes = pl.ds(pl.multiple_of(i * 256, 256), 256)
@@ -594,7 +716,7 @@
         lanes = slice(128 * (i // 2), 128 * (i // 2) + 128)
         rows = [grad_mix[:, lanes], grad_gain_two[:, lanes], *grad_tap, jnp.zeros((11, 128), f32)]
         gc[i // 4, i % 4, 64:80, 0:128] = jnp.concatenate(rows, 0).astype(bf16)
-    conv_g = weight_scatter(gc, 256, 48, gc_a1, gc_a2, gc_b1, gc_b2, gc_a3, gc_a4, gc_b3, gc_b4)
+    conv_g = conv_scatter(gc, gc_r1, gc_r2)
     conv_g[0].start()
     conv_g[1].start()
     scatter_dh1.middle()
@@ -602,12 +724,10 @@
     ffn_g[1].finish()
     ffn_g[2].start()
     ffn_g[3].start()
-    conv_g[0].middle()
-    conv_g[1].middle()
     scatter_out.middle()
 
     d_lifted = scatter_dh1.finish()
-    local = x_ref[...].astype(f32)
+    local = x_ref[0].astype(f32)
     scale_one = lax.rsqrt(jnp.mean(local * local, axis=-1, keepdims=True) + epsilon)
     normed_one = local * scale_one
     scaled = d_lifted * gain_one
@@ -620,8 +740,6 @@
     conv_g[3].start()
     ffn_g[2].middle()
     ffn_g[3].middle()
-    conv_g[2].middle()
-    conv_g[3].middle()
     out_ref[...] = (middle + scatter_out.finish()).astype(bf16)
     conv_g[2].finish()
     conv_g[3].finish()
@@ -653,6 +771,48 @@
     link.drain()
     for scatter in (scatter_r1, scatter_dh2, scatter_out, scatter_dh1):
         scatter.drain()
+
+
+def spread_kernel(
+    block_ref,
+    gin_ref,
+    gff_ref,
+    gwin_ref,
+    gwout_ref,
+    gpack_ref,
+    o_block,
+    o_gin,
+    o_mix,
+    o_in,
+    o_tap,
+    o_proj,
+    o_ffn,
+    o_gate,
+    o_up,
+    o_down,
+):
+    f = lax.axis_index("fsdp")
+    c = lax.axis_index("ctx")
+    lane = lax.broadcasted_iota(jnp.int32, (8, 128), 1)
+    o_block[0] = block_ref[...]
+    o_gin[0] = gin_ref[...]
+    for b in range(3):
+        blocks = [gwin_ref[i, :, 128 * b : 128 * b + 128] for i in range(8)]
+        for v, block in enumerate(by_channel(blocks, lane, True)):
+            o_in[:, 1024 * b + 128 * v : 1024 * b + 128 * v + 128] = block
+    for w in range(8):
+        o_proj[:, 128 * w : 128 * w + 128] = gwout_ref[8 * w : 8 * w + 8]
+    small = gpack_ref[...]
+    gains = pltpu.roll(small, lax.rem(256 - 64 * lax.rem(f, 2) - 8 * c, 128), 1)
+    o_mix[...] = gains[0:1, 0:8]
+    o_ffn[...] = gains[1:2, 0:8]
+    o_tap[...] = pltpu.roll(small, lax.rem(128 - 8 * f, 128), 1)[2:5, 0:8]
+    mixed = gff_ref[:, 1024:1152]
+    o_gate[:, 0:512] = gff_ref[:, 0:512]
+    o_gate[:, 512:576] = mixed[:, 0:64]
+    o_up[:, 0:512] = gff_ref[:, 512:1024]
+    o_up[:, 512:576] = pltpu.roll(mixed, 64, 1)[:, 0:64]
+    o_down[...] = gff_ref[:, 1152:1792].T[0:576]
 
 
 def per_device(
@@ -667,29 +827,9 @@
     down_proj,
     cotangent,
 ):
-    f = lax.axis_index("fsdp")
-    c = lax.axis_index("ctx")
-    wff = jnp.concatenate(
-        [
-            gate_proj[:, :512],
-            up_proj[:, :512],
-            gate_proj[:, 512:],
-            up_proj[:, 512:],
-            down_proj.T,
-            jnp.zeros((64, 64), bf16),
-        ],
-        1,
-    )
-    win = in_proj.reshape(8, 3, 16, 8, 8).transpose(3, 0, 1, 2, 4).reshape(8, 8, 384).astype(f32)
-    wout = out_proj.reshape(8, 8, 128).transpose(1, 0, 2).reshape(64, 128)
-    gains = jnp.stack([mix_gain, ffn_gain], 0).astype(f32)
-    pack = jnp.zeros((8, 128), f32)
-    pack = lax.dynamic_update_slice(pack, gains, (0, 64 * (f % 2) + 8 * c))
-    pack = lax.dynamic_update_slice(pack, conv_kernel.astype(f32), (2, 8 * f))
-
     v = pltpu.VMEM
     in_vmem = pl.BlockSpec(memory_space=pltpu.VMEM)
-    sems = 192
+    sems = 256
     out_shape = (
         jax.ShapeDtypeStruct((128, 1024), bf16),
         jax.ShapeDtypeStruct((128, 1024), f32),
@@ -701,6 +841,8 @@
     scratch = [
         pltpu.SemaphoreType.DMA((sems,)),
         pltpu.SemaphoreType.DMA((sems,)),
+        v((8, 8, 384), f32),
+        v((8, 128), f32),
         v((4, 2, 128, 1024), bf16),
         v((4, 2, 128, 1024), bf16),
         v((4, 2, 128, 1024), bf16),
@@ -736,46 +878,53 @@
         v((2, 64, 896), bf16),
         v((64, 896), bf16),
         v((2, 64, 896), bf16),
-        v((2, 2, CR, 256), bf16),
-        v((2, 4, CR, 256), bf16),
-        v((2, 2, CR, 256), bf16),
-        v((2, 4, CR, 256), bf16),
-        v((CR, 256), bf16),
-        v((2, CR, 256), bf16),
-        v((CR, 256), bf16),
-        v((2, CR, 256), bf16),
+        v((2, 3, 4, CR, 256), bf16),
+        v((2, 3, CR, 256), bf16),
         v((8, 8, 384), f32),
         v((8, 8, 384), f32),
         v((8, 128), f32),
         v((7, 8, 128), f32),
     ]
-    block_out, grad_inputs, gff, gwin, gwout, gpack = pl.pallas_call(
+    raw = pl.pallas_call(
         block_kernel,
         out_shape=out_shape,
-        in_specs=[in_vmem] * 6,
+        in_specs=[in_vmem] * 10,
         out_specs=(in_vmem,) * 6,
         scratch_shapes=scratch,
         compiler_params=pltpu.CompilerParams(
             collective_id=0, has_side_effects=True, vmem_limit_bytes=62 * 1024 * 1024
         ),
-    )(inputs.reshape(128, 1024), cotangent.reshape(128, 1024), wff, win, wout, pack)
-
-    grad_gains = lax.dynamic_slice(gpack, (0, 64 * (f % 2) + 8 * c), (2, 8))
-    grad_taps = lax.dynamic_slice(gpack, (2, 8 * f), (3, 8))
-    grad_in = gwin.reshape(8, 8, 3, 16, 8).transpose(1, 2, 3, 0, 4).reshape(8, 3072)
-    grad_out = gwout.reshape(8, 8, 128).transpose(1, 0, 2).reshape(8, 1024)
-    return (
-        block_out.reshape(inputs.shape),
-        grad_inputs.reshape(inputs.shape),
-        grad_gains[0],
-        grad_in,
-        grad_taps,
-        grad_out,
-        grad_gains[1],
-        jnp.concatenate([gff[:, :512], gff[:, 1024:1088]], 1),
-        jnp.concatenate([gff[:, 512:1024], gff[:, 1088:1152]], 1),
-        gff[:, 1152:1728].T,
+    )(
+        inputs,
+        cotangent,
+        mix_gain.reshape(1, 8),
+        in_proj,
+        conv_kernel,
+        out_proj,
+        ffn_gain.reshape(1, 8),
+        gate_proj,
+        up_proj,
+        down_proj,
     )
+    made = pl.pallas_call(
+        spread_kernel,
+        out_shape=(
+            jax.ShapeDtypeStruct(inputs.shape, bf16),
+            jax.ShapeDtypeStruct(inputs.shape, f32),
+            jax.ShapeDtypeStruct((1, 8), f32),
+            jax.ShapeDtypeStruct(in_proj.shape, f32),
+            jax.ShapeDtypeStruct(conv_kernel.shape, f32),
+            jax.ShapeDtypeStruct(out_proj.shape, f32),
+            jax.ShapeDtypeStruct((1, 8), f32),
+            jax.ShapeDtypeStruct(gate_proj.shape, f32),
+            jax.ShapeDtypeStruct(up_proj.shape, f32),
+            jax.ShapeDtypeStruct(down_proj.shape, f32),
+        ),
+        in_specs=[in_vmem] * 6,
+        out_specs=(in_vmem,) * 10,
+        compiler_params=pltpu.CompilerParams(vmem_limit_bytes=16 * 1024 * 1024),
+    )(*raw)
+    return (*made[:2], made[2].reshape(8), *made[3:6], made[6].reshape(8), *made[7:])
 
 
 def solution(mesh):

time: 166 us -> 147 us (0.89)
  local copies, waits for them, and re-layouts: 18.5 us -> 7.81 us
  Pallas kernels: 145 us -> 138 us
    pallas_call x1 -> x2, Pallas kernels: 145 us -> 138 us  [the longest x1 136 us: per_device(): pl.pallas_call(block_kernel, out_shape=out_shape, in_specs=[in_vmem] * 10...]
    unnamed x21 -> x14, local copies, waits for them, and re-layouts: 2.74 us -> 7.81 us
    convert_element_type x3 -> x0, local copies, waits for them, and re-layouts: 3.33 us -> none  [per_device(): in_proj.reshape(8, 3, 16, 8, 8).transpose(3, 0, 1, 2, 4).reshape(8, 8, 384)]
    slice x6 -> x0, local copies, waits for them, and re-layouts: 3.22 us -> none  [the longest x1 0.85 us: per_device(): gate_proj[:, :512]]
    reshape x2 -> x0, local copies, waits for them, and re-layouts: 3.21 us -> none  [per_device(): gwin.reshape(8, 8, 3, 16, 8).transpose(1, 2, 3, 0, 4).reshape(8, 3072)]
    concatenate x1 -> x0, local copies, waits for them, and re-layouts: 1.67 us -> none  [per_device(): jnp.concatenate([gate_proj[:, :512], up_proj[:, :512], gate_proj[:, 512:]...]
where the time goes in v2:
time: 147 us; the launch traced here: 146 us
  Pallas kernels  138 us (94%)
  local copies, waits for them, and re-layouts  7.81 us (5%)
    pallas_call x1, Pallas kernels, per_device(): pl.pallas_call(block_kernel, out_shape=out_shape, in_specs=[in_vmem] * 10...  136 us
    unnamed x14, local copies, waits for them, and re-layouts  7.81 us

profile of v2, /device:TPU:1, one launch (start us, length us, event | category | flops | bytes accessed | tf_op | source)
XLA Modules:
  0.0 146.2 jit_solution(18304948333678927332)
XLA Ops:
  0.6 1.7 %copy.20.down_ref = bf16[576,64]{1,0:T(8,128)(2,1)} copy(bf16[576,64]{0,1:T(8,128)(2,1)} %param.18) | data formatting | bytes 147456 | tf_op args[8]
  2.3 136.2 %shard_map.177 = (bf16[128,1024]{1,0:T(8,128)(2,1)}, f32[128,1024]{1,0:T(8,128)}, f32[64,1792]{1,0:T(8,128)}, f32[8,8,384]{2,1,0:T(8,128)}, f32[64,128]{1,0:T(8,128)}, /*index=5*/f32[8,128]{1,0:T(8,128)}) custom-call(bf16[1,128,1024]{2,1,0:T(8,128)(2,1)} %x_ref.1, bf16[1,128,1024]{2,1,0:T(8,128)(2,1)} %cot_ref.1, bf16[1,8]{1,0:T(2,128)(2,1)} %bitcast.4, ...), custom_call_target="tpu_custom_call" | custom-call | tf_op jit(solution)/shard_map/pallas_call | solution.py:888
  138.5 0.0 copy-start.5
  138.6 0.7 copy-done.5
  139.2 0.0 copy-start
  139.2 1.0 copy-done
  140.3 0.0 copy-start.1
  140.3 1.0 copy-done.1
  141.3 0.0 copy-start.2
  141.3 0.9 copy-done.2
  142.2 0.0 copy-start.3
  142.2 0.9 copy-done.3
  143.1 0.0 copy-start.4
  143.1 0.8 copy-done.4
  143.9 1.5 %shard_map.178 = (bf16[1,128,1024]{2,1,0:T(8,128)(2,1)}, f32[1,128,1024]{2,1,0:T(8,128)}, f32[1,8]{1,0:T(1,128)}, f32[8,3072]{1,0:T(8,128)}, f32[3,8]{1,0:T(4,12...) custom-call(bf16[128,1024]{1,0:T(8,128)(2,1)S(1)} %copy-done.2, ...), custom_call_target="tpu_custom_call" | custom-call | tf_op jit(solution)/shard_map/pallas_call | solution.py:909
  145.4 0.8 copy.21
Async XLA Ops:
  138.5 0.7 copy-start.5
  139.2 1.0 copy-start
  140.3 1.0 copy-start.1
  141.3 0.9 copy-start.2
  142.2 0.9 copy-start.3
  143.1 0.8 copy-start.4

commit v3 on v2

--- a/solution.py
+++ b/solution.py
@@ -161,6 +161,8 @@
     def __init__(self, link, buf, y, core, plus, minus, other):
         self.link, self.buf, self.y, self.core = link, buf, y, core
         self.plus, self.minus, self.other = plus, minus, other
+        self.left, self.far, self.right = ring(y, 3), ring(y, 2), ring(y, 1)
+        self.mate = 1 - core
 
     def half(self, which, part):
         return self.buf.at[which, self.core, (LO, HI)[part]]
@@ -178,26 +180,26 @@
         half = self.half(which, part)
         self.link.landed(handle, half)
         onward = None if device is None else self.link.send(half, half, device)
-        theirs = self.buf.at[which, 1 - self.core, (LO, HI)[part]]
+        theirs = self.buf.at[which, self.mate, (LO, HI)[part]]
         self.late.append((self.link.send(half, half, self.other), theirs))
         return onward
 
     def forward(self):
-        left, right = ring(self.y, 3), ring(self.y, 1)
+        left, right = self.left, self.right
         self.fp = self.pass_on(self.p0, left, 0, self.plus)
         self.fm = self.pass_on(self.m1, right, 1, self.minus)
 
     def sides(self):
-        self.pass_on(self.p1, ring(self.y, 3), 1, None)
-        self.pass_on(self.m0, ring(self.y, 1), 0, None)
+        self.pass_on(self.p1, self.left, 1, None)
+        self.pass_on(self.m0, self.right, 0, None)
 
     def across(self):
-        far = ring(self.y, 2)
+        far = self.far
         self.pass_on(self.fp, far, 0, None)
         self.pass_on(self.fm, far, 1, None)
 
     def finish_near(self):
-        self.link.landed(self.near, self.buf.at[self.y, 1 - self.core])
+        self.link.landed(self.near, self.buf.at[self.y, self.mate])
 
     def finish_far(self):
         for handle, ref in self.late:
@@ -205,19 +207,24 @@
 
 
 class CtxScatter:
-    def __init__(self, link, part, rb, r1, r2, y, core, plus, minus, other):
+    def __init__(self, link, part, rb, r1, r2, y, core, plus, minus, other, own_first):
         self.link, self.part, self.rb, self.r1, self.r2 = link, part, rb, r1, r2
-        self.y, self.core = y, core
+        self.y, self.core, self.own_first = y, core, own_first
         self.plus, self.minus, self.other = plus, minus, other
+        self.left, self.far, self.right = ring(y, 3), ring(y, 2), ring(y, 1)
+        self.mate = 1 - core
         self.first = link.reserve(4)
+        self.at_far, self.at_left, self.at_right, self.at_own = (1, 2, 3, 0) if own_first else (0, 1, 2, 3)
 
     def group(self, step):
+        if self.own_first:
+            return lax.rem(self.y + 2 * step - step // 2, 4)
         return lax.rem(self.y + 2 + step + step // 2 + 2 * (step // 3), 4)
 
     def cross(self, step):
         g = self.group(step)
         self.link.copy(
-            self.part.at[g, 1 - self.core], self.rb.at[g], self.other, self.first + step
+            self.part.at[g, self.mate], self.rb.at[g], self.other, self.first + step
         ).start()
 
     def crossed(self, g, step):
@@ -228,24 +235,24 @@
         return self.part.at[which, self.core, rows]
 
     def start(self):
-        far = ring(self.y, 2)
-        self.crossed(far, 0)
+        far = self.far
+        self.crossed(far, self.at_far)
         add_into(self.block(far, LO), self.rb.at[far, LO])
         self.h1a = self.link.send(self.block(far, LO), self.r1.at[0], self.plus)
         add_into(self.block(far, HI), self.rb.at[far, HI])
         self.h1b = self.link.send(self.block(far, HI), self.r1.at[1], self.minus)
 
     def sides(self):
-        left, right = ring(self.y, 3), ring(self.y, 1)
-        self.crossed(left, 1)
+        left, right = self.left, self.right
+        self.crossed(left, self.at_left)
         add_into(self.block(left, LO), self.rb.at[left, LO])
         self.h2b0 = self.link.send(self.block(left, LO), self.r2.at[1, LO], self.minus)
-        self.crossed(right, 2)
+        self.crossed(right, self.at_right)
         add_into(self.block(right, HI), self.rb.at[right, HI])
         self.h2a1 = self.link.send(self.block(right, HI), self.r2.at[0, HI], self.plus)
 
     def middle(self):
-        left, right = ring(self.y, 3), ring(self.y, 1)
+        left, right = self.left, self.right
         self.link.landed(self.h1a, self.r1.at[0])
         add_into(self.block(right, LO), self.rb.at[right, LO], self.r1.at[0])
         self.h2a0 = self.link.send(self.block(right, LO), self.r2.at[0, LO], self.plus)
@@ -254,7 +261,7 @@
         self.h2b1 = self.link.send(self.block(left, HI), self.r2.at[1, HI], self.minus)
 
     def finish(self):
-        self.crossed(self.y, 3)
+        self.crossed(self.y, self.at_own)
         self.link.landed(self.h2b0, self.r2.at[1, LO])
         self.link.landed(self.h2a1, self.r2.at[0, HI])
         self.link.landed(self.h2a0, self.r2.at[0, LO])
@@ -269,7 +276,7 @@
     def drain(self):
         for step in range(4):
             g = self.group(step)
-            src = self.part.at[g, 1 - self.core]
+            src = self.part.at[g, self.mate]
             self.link.copy(src, src, self.other, self.first + step).wait_send()
 
 
@@ -290,6 +297,22 @@
 
 
 def block_kernel(
+    x_hbm,
+    cot_hbm,
+    mix_hbm,
+    in_hbm,
+    tap_hbm,
+    proj_hbm,
+    ffn_hbm,
+    gate_hbm,
+    up_hbm,
+    down_hbm,
+    out_hbm,
+    gin_hbm,
+    gff_hbm,
+    gwin_hbm,
+    gwout_hbm,
+    gpack_hbm,
     x_ref,
     cot_ref,
     mix_ref,
@@ -306,6 +329,7 @@
     gwin_ref,
     gwout_ref,
     gpack_ref,
+    local_sems,
     send_sems,
     recv_sems,
     win_ref,
@@ -319,13 +343,16 @@
     pre_in,
     pre_pack,
     w_in,
-    w_out,
+    wog,
     h1g,
     scale_g,
     proj,
     bx_pad,
     z_buf,
     y_buf,
+    y_own,
+    dy_buf,
+    dy_own,
     hid_buf,
     dgu_buf,
     dz_pad,
@@ -347,11 +374,32 @@
     gf_b4,
     gc_r1,
     gc_r2,
+    gc_r3,
+    gc_r4,
     post_send,
     post_in,
     post_own,
     post_pack,
 ):
+    loads = [
+        pltpu.make_async_copy(src, dst, local_sems.at[i])
+        for i, (src, dst) in enumerate(
+            (
+                (x_hbm, x_ref),
+                (in_hbm, in_ref),
+                (mix_hbm, mix_ref),
+                (ffn_hbm, ffn_ref),
+                (tap_hbm, tap_ref),
+                (proj_hbm, proj_ref),
+                (gate_hbm, gate_ref),
+                (up_hbm, up_ref),
+                (down_hbm, down_ref),
+                (cot_hbm, cot_ref),
+            )
+        )
+    ]
+    for load in loads:
+        load.start()
     f = lax.axis_index("fsdp")
     c = lax.axis_index("ctx")
     z, x = f // 4, lax.rem(f, 4)
@@ -376,6 +424,8 @@
 
     lane = lax.broadcasted_iota(jnp.int32, (8, 128), 1)
     row = lax.broadcasted_iota(jnp.int32, (8, 128), 0)
+    for load in loads[:5]:
+        load.wait()
     xg[y, core] = x_ref[0]
     in_rows = in_ref[...].astype(f32)
     for b in range(3):
@@ -398,11 +448,18 @@
     def ctx_gather(buf):
         return CtxGather(link, buf, y, core, y_plus, y_minus, other)
 
-    def ctx_scatter(n):
+    def ctx_scatter(n, own_first=False):
         return CtxScatter(
             link, rs_part.at[n], rs_rb.at[n], rs_r1.at[n], rs_r2.at[n],
-            y, core, y_plus, y_minus, other,
-        )
+            y, core, y_plus, y_minus, other, own_first,
+        )
+
+    def exchange(blocks, landing):
+        return [link.send(blocks.at[mate[1]], landing.at[c], mate) for mate in mates]
+
+    def exchanged(handles, landing):
+        for step, handle in enumerate(handles):
+            link.landed(handle, landing.at[lax.rem(c + 7 - step, 8)])
 
     def weight_gather(buf, half, low):
         rest = buf.shape[3] - half
@@ -431,13 +488,16 @@
             DirectGather(link, lambda i, p: buf.at[:, i, :, b], x, along_x),
         )
 
-    def conv_scatter(buf, r1, r2):
-        a, b = pl.ds(0, 256), pl.ds(256, 256)
+    def conv_scatter(buf, r1, r2, r3, r4):
+        a, b, o = pl.ds(0, 256), pl.ds(256, 128), pl.ds(384, 128)
+        rows = pl.ds(0, 64)
         return (
-            DirectScatter(link, lambda i, p: buf.at[i, :, :, a], z, along_z, r1.at[0]),
-            DirectScatter(link, lambda i, p: buf.at[:, i, :, b], x, along_x, r1.at[1]),
-            DirectScatter(link, lambda i, p: buf.at[z, i, :, a], x, along_x, r2.at[0]),
-            DirectScatter(link, lambda i, p: buf.at[i, x, :, b], z, along_z, r2.at[1]),
+            DirectScatter(link, lambda i, p: buf.at[i, :, :, a], z, along_z, r1),
+            DirectScatter(link, lambda i, p: buf.at[:, i, rows, b], x, along_x, r2.at[0]),
+            DirectScatter(link, lambda i, p: buf.at[z, i, :, a], x, along_x, r3),
+            DirectScatter(link, lambda i, p: buf.at[i, x, rows, b], z, along_z, r4.at[0]),
+            DirectScatter(link, lambda i, p: buf.at[:, i, rows, o], x, along_x, r2.at[1]),
+            DirectScatter(link, lambda i, p: buf.at[i, x, rows, o], z, along_z, r4.at[1]),
         )
 
     def weight_scatter(buf, half, low, a1, a2, b1, b2, a3, a4, b3, b4):
@@ -473,13 +533,15 @@
         )
     gather_x = ctx_gather(xg)
     gather_x.start()
+    for load in loads[5:]:
+        load.wait()
     own = wf.at[z, x]
     own[:, 0:512] = gate_ref[:, 0:512]
     own[:, 512:1024] = up_ref[:, 0:512]
     own[:, 1024:1152] = jnp.concatenate([gate_ref[:, 512:576], up_ref[:, 512:576]], 1)
     own[:, 1152:1792] = jnp.concatenate(
-        [down_ref[...].astype(f32).T, jnp.zeros((64, 64), f32)], 1
-    ).astype(bf16)
+        [down_ref[...], jnp.zeros((64, 64), bf16)], 1
+    )
     cotg[y, core] = cot_ref[0]
     out_rows = proj_ref[...].astype(f32)
     wc[z, x, 0:64, 384:512] = jnp.concatenate(
@@ -514,12 +576,19 @@
     gather_x.finish_far()
     gather_cot = ctx_gather(cotg)
     gather_cot.start()
-    conv_w[2].finish()
-    conv_w[3].finish()
     ffn_w[0].finish()
     ffn_w[1].finish()
     ffn_w[2].start()
     ffn_w[3].start()
+
+    def first_scale(g, carry):
+        values = xg[g].reshape(256, 1024).astype(f32)
+        scale_g[g] = lax.rsqrt(jnp.mean(values * values, axis=-1, keepdims=True) + epsilon)
+        return carry
+
+    lax.fori_loop(0, 4, first_scale, 0)
+    conv_w[2].finish()
+    conv_w[3].finish()
 
     packs = [wc[i // 4, i % 4, 64:80, 0:128].astype(f32)[0:8] for i in range(16)]
     gain_one = jnp.concatenate([packs[2 * w][0:1] + packs[2 * w + 1][0:1] for w in range(8)], 1)
@@ -531,13 +600,13 @@
     w_in[...] = wc[:, :, 0:64, 0:384].reshape(1024, 384)
     slab = wc[:, :, 0:64, 384:512].astype(f32).reshape(16, 8, 8, 128)
     for w in range(8):
-        w_out[:, 128 * w : 128 * w + 128] = slab[:, w].reshape(128, 128).astype(bf16)
+        wog[y, core, :, 128 * w : 128 * w + 128] = slab[:, w].reshape(128, 128).astype(bf16)
+    gather_out = ctx_gather(wog)
+    gather_out.start()
 
     def project(g, carry):
         values = xg[g].reshape(256, 1024).astype(f32)
-        scale = lax.rsqrt(jnp.mean(values * values, axis=-1, keepdims=True) + epsilon)
-        scale_g[g] = scale
-        lifted = (values * scale * gain_one).astype(bf16)
+        lifted = (values * scale_g[g] * gain_one).astype(bf16)
         h1g[g] = lifted
         proj[g] = mm(lifted, w_in[...])
         return carry
@@ -549,26 +618,22 @@
     bx_pad[8:1032] = (b_part * x_part).astype(bf16).astype(f32)
     z_all = tap[0] * bx_pad[6:1030] + tap[1] * bx_pad[7:1031] + tap[2] * bx_pad[8:1032]
     z_buf[...] = z_all
-    y_buf[...] = (proj[:, :, 128:256].reshape(1024, 128) * z_all).astype(bf16).reshape(4, 256, 128)
+    y_buf[...] = (proj[:, :, 128:256].reshape(1024, 128) * z_all).astype(bf16).reshape(8, 128, 128)
+    swap_y = exchange(y_buf, y_own)
+    y_own[c] = y_buf[c]
     gather_cot.forward()
+    gather_out.forward()
     gather_cot.sides()
+    gather_out.sides()
+    gather_cot.across()
+    gather_out.across()
     ffn_w[2].forward()
     ffn_w[3].forward()
-
-    scatter_r1 = ctx_scatter(0)
-
-    def branch_out(step, carry):
-        g = scatter_r1.group(step)
-        rs_part[0, g] = mm(y_buf[g], w_out[...]).astype(bf16).reshape(2, 128, 1024)
-        scatter_r1.cross(step)
-        return carry
-
-    lax.fori_loop(0, 4, branch_out, 0)
-    scatter_r1.start()
-    scatter_r1.sides()
-    scatter_r1.middle()
-    gather_cot.across()
-    middle = x_ref[0].astype(f32) + scatter_r1.finish()
+    exchanged(swap_y, y_own)
+    gather_out.finish_near()
+    gather_out.finish_far()
+    gated = jnp.concatenate([y_own[i] for i in range(8)], 1)
+    middle = x_ref[0].astype(f32) + mm(gated, wog[...].reshape(1024, 1024))
     scale_two = lax.rsqrt(jnp.mean(middle * middle, axis=-1, keepdims=True) + epsilon)
     h2g[y, core] = (middle * scale_two * gain_two).astype(bf16)
     gather_h2 = ctx_gather(h2g)
@@ -577,17 +642,25 @@
     gather_cot.finish_far()
     ffn_w[2].finish()
     ffn_w[3].finish()
-    gather_h2.forward()
-    gather_h2.sides()
-    gather_h2.across()
     gather_h2.finish_near()
-    gather_h2.finish_far()
-
-    scatter_dh2 = ctx_scatter(1)
+
+    scatter_dh2 = ctx_scatter(0, own_first=True)
     low_half = lax.broadcasted_iota(jnp.int32, (256, 128), 1) < 64
 
     def feed_forward(step, carry):
         g = scatter_dh2.group(step)
+
+        @pl.when(step == 1)
+        def _():
+            gather_h2.forward()
+            gather_h2.sides()
+            gather_h2.across()
+            gather_h2.finish_far()
+
+        @pl.when(step == 2)
+        def _():
+            scatter_dh2.start()
+
         w_gu = wf[:, :, :, 0:GU].reshape(1024, GU)
         gu = mm(h2g[g].reshape(256, 1024), w_gu)
         mixed = gu[:, 1024:1152]
@@ -605,33 +678,40 @@
         d_mixed = jnp.where(low_half, d_gating[:, 512:640], pltpu.roll(d_upward[:, 512:640], 64, 1))
         d_gu = jnp.concatenate([d_gating[:, 0:512], d_upward[:, 0:512], d_mixed], 1).astype(bf16)
         dgu_buf[g] = d_gu
-        rs_part[1, g] = mt(d_gu, w_gu).astype(bf16).reshape(2, 128, 1024)
+        rs_part[0, g] = mt(d_gu, w_gu).astype(bf16).reshape(2, 128, 1024)
         scatter_dh2.cross(step)
         return carry
 
     lax.fori_loop(0, 4, feed_forward, 0)
-    scatter_dh2.start()
     scatter_dh2.sides()
-
-    scatter_out = ctx_scatter(2)
+    scatter_out = ctx_scatter(1)
 
     def ffn_out(step, carry):
         g = scatter_out.group(step)
         w_down = wf[:, :, :, GU:FFL].reshape(1024, HID)
-        rs_part[2, g] = mt(hid_buf[g], w_down).astype(bf16).reshape(2, 128, 1024)
+        rs_part[1, g] = mt(hid_buf[g], w_down).astype(bf16).reshape(2, 128, 1024)
         scatter_out.cross(step)
         return carry
 
     lax.fori_loop(0, 4, ffn_out, 0)
     scatter_dh2.middle()
-
-    def grad_gu(i, carry):
+    scatter_out.start()
+    scatter_out.sides()
+
+    def grad_ffn(i, carry):
         lanes = pl.ds(pl.multiple_of(i * 256, 256), 256)
         lhs = h2g[:, :, :, lanes].reshape(1024, 256)
         gf[i, :, :, 0:GU] = tm(lhs, dgu_buf[...].reshape(1024, GU)).astype(bf16).reshape(4, 64, GU)
+        lhs = cotg[:, :, :, lanes].reshape(1024, 256)
+        gf[i, :, :, GU:FFL] = (
+            tm(lhs, hid_buf[...].reshape(1024, HID)).astype(bf16).reshape(4, 64, HID)
+        )
         return carry
 
-    lax.fori_loop(0, 2, grad_gu, 0)
+    lax.fori_loop(0, 4, grad_ffn, 0)
+    ffn_g = weight_scatter(gf, 896, 32, gf_a1, gf_a2, gf_b1, gf_b2, gf_a3, gf_a4, gf_b3, gf_b4)
+    ffn_g[0].start()
+    ffn_g[1].start()
 
     d_second = scatter_dh2.finish()
     normed_two = middle * scale_two
@@ -640,36 +720,22 @@
     d_middle = cot_ref[0].astype(f32) + scale_two * (
         scaled - normed_two * jnp.mean(scaled * normed_two, axis=-1, keepdims=True)
     )
-    dg[y, core] = d_middle.astype(bf16)
+    d_branch = d_middle.astype(bf16)
+    dg[y, core] = d_branch
+    d_gated = mt(d_branch, wog[...].reshape(1024, 1024)).astype(bf16)
+    for i in range(8):
+        dy_buf[i] = d_gated[:, 128 * i : 128 * i + 128]
+    swap_dy = exchange(dy_buf, dy_own)
     gather_d = ctx_gather(dg)
     gather_d.start()
-
-    lax.fori_loop(2, 4, grad_gu, 0)
-    gather_d.forward()
-    gather_d.sides()
-
-    def grad_down(i, carry):
-        lanes = pl.ds(pl.multiple_of(i * 256, 256), 256)
-        lhs = cotg[:, :, :, lanes].reshape(1024, 256)
-        gf[i, :, :, GU:FFL] = (
-            tm(lhs, hid_buf[...].reshape(1024, HID)).astype(bf16).reshape(4, 64, HID)
-        )
-        return carry
-
-    lax.fori_loop(0, 4, grad_down, 0)
-    ffn_g = weight_scatter(gf, 896, 32, gf_a1, gf_a2, gf_b1, gf_b2, gf_a3, gf_a4, gf_b3, gf_b4)
-    ffn_g[0].start()
-    ffn_g[1].start()
-    gather_d.across()
-    scatter_out.start()
-    scatter_out.sides()
-    gather_d.finish_near()
-    gather_d.finish_far()
-
-    for g in range(4):
-        d_gated = mt(dg[g].reshape(256, 1024), w_out[...])
-        dz_pad[256 * g : 256 * g + 256] = d_gated * proj[g, :, 128:256]
-        dp_buf[g, :, 128:256] = (d_gated * z_buf[256 * g : 256 * g + 256]).astype(bf16)
+    dy_own[c] = dy_buf[c]
+    ffn_g[0].middle()
+    ffn_g[1].middle()
+    exchanged(swap_dy, dy_own)
+
+    d_gated = dy_own[...].reshape(1024, 128).astype(f32)
+    dz_pad[0:1024] = d_gated * proj[:, :, 128:256].reshape(1024, 128)
+    dp_buf[:, :, 128:256] = (d_gated * z_buf[...]).astype(bf16).reshape(4, 256, 128)
     dz_pad[1024:1032] = jnp.zeros((8, 128), f32)
     d_bx = tap[2] * dz_pad[0:1024] + tap[1] * dz_pad[1:1025] + tap[0] * dz_pad[2:1026]
     d_bx = d_bx.reshape(4, 256, 128)
@@ -678,16 +744,16 @@
     grad_tap = [
         jnp.sum(dz_pad[0:1024] * bx_pad[6 + k : 1030 + k], axis=0, keepdims=True) for k in range(3)
     ]
-    ffn_g[0].middle()
-    ffn_g[1].middle()
-
-    scatter_dh1 = ctx_scatter(3)
+    gather_d.forward()
+    gather_d.sides()
+
+    scatter_dh1 = ctx_scatter(2)
     mix_acc[...] = jnp.zeros((8, 1024), f32)
 
     def branch_back(step, carry):
         g = scatter_dh1.group(step)
         d_lifted = mt(dp_buf[g], w_in[...])
-        rs_part[3, g] = d_lifted.astype(bf16).reshape(2, 128, 1024)
+        rs_part[2, g] = d_lifted.astype(bf16).reshape(2, 128, 1024)
         scatter_dh1.cross(step)
         normed = xg[g].reshape(256, 1024).astype(f32) * scale_g[g]
         mix_acc[...] += jnp.sum((d_lifted * normed).reshape(32, 8, 1024), axis=0)
@@ -707,24 +773,34 @@
 
     lax.fori_loop(0, 4, grad_in, 0)
     grad_mix = jnp.sum(mix_acc[...], axis=0, keepdims=True)
-    g_out = tm(y_buf[...].reshape(1024, 128), dg[...].reshape(1024, 1024))
-    pieces = [g_out[:, 128 * w : 128 * w + 128].reshape(16, 1, 8, 128) for w in range(8)]
-    g_slab = jnp.concatenate(pieces, 1).reshape(4, 4, 64, 128)
-    gc[:, :, 0:64, 384:512] = g_slab.astype(bf16)
     gc[:, :, 64:80, 128:512] = jnp.zeros((4, 4, 16, 384), bf16)
     for i in range(16):
         lanes = slice(128 * (i // 2), 128 * (i // 2) + 128)
         rows = [grad_mix[:, lanes], grad_gain_two[:, lanes], *grad_tap, jnp.zeros((11, 128), f32)]
         gc[i // 4, i % 4, 64:80, 0:128] = jnp.concatenate(rows, 0).astype(bf16)
-    conv_g = conv_scatter(gc, gc_r1, gc_r2)
-    conv_g[0].start()
-    conv_g[1].start()
+    conv_g = conv_scatter(gc, gc_r1, gc_r2, gc_r3, gc_r4)
+    for part in conv_g[0:2]:
+        part.start()
     scatter_dh1.middle()
+    gather_d.across()
+    gather_d.finish_near()
+    gather_d.finish_far()
+    g_out = tm(y_buf[...].reshape(1024, 128), dg[...].reshape(1024, 1024))
+    pieces = [g_out[:, 128 * w : 128 * w + 128].reshape(16, 1, 8, 128) for w in range(8)]
+    g_slab = jnp.concatenate(pieces, 1).reshape(4, 4, 64, 128)
+    gc[:, :, 0:64, 384:512] = g_slab.astype(bf16)
+    conv_g[4].start()
     ffn_g[0].finish()
     ffn_g[1].finish()
     ffn_g[2].start()
     ffn_g[3].start()
+    for part in conv_g[0:2]:
+        part.finish()
+    for part in conv_g[2:4]:
+        part.start()
     scatter_out.middle()
+    conv_g[4].finish()
+    conv_g[5].start()
 
     d_lifted = scatter_dh1.finish()
     local = x_ref[0].astype(f32)
@@ -734,19 +810,27 @@
     gin_ref[...] = d_middle + scale_one * (
         scaled - normed_one * jnp.mean(scaled * normed_one, axis=-1, keepdims=True)
     )
-    conv_g[0].finish()
-    conv_g[1].finish()
-    conv_g[2].start()
-    conv_g[3].start()
+    stores = [
+        pltpu.make_async_copy(src, dst, local_sems.at[10 + i])
+        for i, (src, dst) in enumerate(
+            (
+                (gin_ref, gin_hbm),
+                (gff_ref, gff_hbm),
+                (out_ref, out_hbm),
+                (gwout_ref, gwout_hbm),
+                (gwin_ref, gwin_hbm),
+                (gpack_ref, gpack_hbm),
+            )
+        )
+    ]
+    stores[0].start()
     ffn_g[2].middle()
     ffn_g[3].middle()
-    out_ref[...] = (middle + scatter_out.finish()).astype(bf16)
-    conv_g[2].finish()
-    conv_g[3].finish()
-
-    total = gc[z, x].astype(f32)
-    gwout_ref[...] = total[0:64, 384:512]
-    post_send[...] = total[0:64, 0:384].reshape(8, 8, 384)
+    for part in conv_g[2:4]:
+        part.finish()
+
+    total = gc[z, x, :, 0:384].astype(f32)
+    post_send[...] = total[0:64].reshape(8, 8, 384)
     post_own[...] = total[64:72, 0:128]
     post = []
     for step, mate in enumerate(mates):
@@ -759,6 +843,12 @@
     ffn_g[2].finish()
     ffn_g[3].finish()
     gff_ref[...] = gf[z, x].astype(f32)
+    stores[1].start()
+    out_ref[...] = (middle + scatter_out.finish()).astype(bf16)
+    stores[2].start()
+    conv_g[5].finish()
+    gwout_ref[...] = gc[z, x, 0:64, 384:512].astype(f32)
+    stores[3].start()
     post_in[c] = post_send[c]
     summed = post_own[...]
     for step, (h_in, h_pack) in enumerate(post):
@@ -767,9 +857,13 @@
         summed = summed + post_pack[step]
     gwin_ref[...] = post_in[...]
     gpack_ref[...] = jnp.where(row < 2, summed, post_own[...])
+    stores[4].start()
+    stores[5].start()
+    for store in stores:
+        store.wait()
 
     link.drain()
-    for scatter in (scatter_r1, scatter_dh2, scatter_out, scatter_dh1):
+    for scatter in (scatter_dh2, scatter_out, scatter_dh1):
         scatter.drain()
 
 
@@ -812,7 +906,7 @@
     o_gate[:, 512:576] = mixed[:, 0:64]
     o_up[:, 0:512] = gff_ref[:, 512:1024]
     o_up[:, 512:576] = pltpu.roll(mixed, 64, 1)[:, 0:64]
-    o_down[...] = gff_ref[:, 1152:1792].T[0:576]
+    o_down[...] = gff_ref[:, 1152:1728]
 
 
 def per_device(
@@ -828,7 +922,7 @@
     cotangent,
 ):
     v = pltpu.VMEM
-    in_vmem = pl.BlockSpec(memory_space=pltpu.VMEM)
+    anywhere = pl.BlockSpec(memory_space=pl.ANY)
     sems = 256
     out_shape = (
         jax.ShapeDtypeStruct((128, 1024), bf16),
@@ -839,6 +933,18 @@
         jax.ShapeDtypeStruct((8, 128), f32),
     )
     scratch = [
+        v(inputs.shape, bf16),
+        v(cotangent.shape, bf16),
+        v((1, 8), bf16),
+        v(in_proj.shape, bf16),
+        v(conv_kernel.shape, bf16),
+        v(out_proj.shape, bf16),
+        v((1, 8), bf16),
+        v(gate_proj.shape, bf16),
+        v(up_proj.shape, bf16),
+        v(down_proj.shape[::-1], bf16),
+        *[v(shape.shape, shape.dtype) for shape in out_shape],
+        pltpu.SemaphoreType.DMA((16,)),
         pltpu.SemaphoreType.DMA((sems,)),
         pltpu.SemaphoreType.DMA((sems,)),
         v((8, 8, 384), f32),
@@ -852,22 +958,25 @@
         v((8, 8, 384), f32),
         v((7, 8, 128), f32),
         v((1024, 384), bf16),
-        v((128, 1024), bf16),
+        v((4, 2, 128, 1024), bf16),
         v((4, 256, 1024), bf16),
         v((4, 256, 1), f32),
         v((4, 256, 384), f32),
         v((1032, 128), f32),
         v((1024, 128), f32),
-        v((4, 256, 128), bf16),
+        v((8, 128, 128), bf16),
+        v((8, 128, 128), bf16),
+        v((8, 128, 128), bf16),
+        v((8, 128, 128), bf16),
         v((4, 256, HID), bf16),
         v((4, 256, GU), bf16),
         v((1032, 128), f32),
         v((4, 256, 384), bf16),
         v((8, 1024), f32),
-        v((4, 4, 2, 128, 1024), bf16),
-        v((4, 4, 128, 1024), bf16),
-        v((4, 2, 64, 1024), bf16),
-        v((4, 2, 128, 1024), bf16),
+        v((3, 4, 2, 128, 1024), bf16),
+        v((3, 4, 128, 1024), bf16),
+        v((3, 2, 64, 1024), bf16),
+        v((3, 2, 128, 1024), bf16),
         v((4, 4, 64, FFL), bf16),
         v((4, 4, CR, CL), bf16),
         v((2, 2, 64, 896), bf16),
@@ -878,8 +987,10 @@
         v((2, 64, 896), bf16),
         v((64, 896), bf16),
         v((2, 64, 896), bf16),
-        v((2, 3, 4, CR, 256), bf16),
-        v((2, 3, CR, 256), bf16),
+        v((3, 4, CR, 256), bf16),
+        v((2, 3, 4, 64, 128), bf16),
+        v((3, CR, 256), bf16),
+        v((2, 3, 64, 128), bf16),
         v((8, 8, 384), f32),
         v((8, 8, 384), f32),
         v((8, 128), f32),
@@ -888,8 +999,8 @@
     raw = pl.pallas_call(
         block_kernel,
         out_shape=out_shape,
-        in_specs=[in_vmem] * 10,
-        out_specs=(in_vmem,) * 6,
+        in_specs=[anywhere] * 10,
+        out_specs=(anywhere,) * 6,
         scratch_shapes=scratch,
         compiler_params=pltpu.CompilerParams(
             collective_id=0, has_side_effects=True, vmem_limit_bytes=62 * 1024 * 1024
@@ -904,7 +1015,7 @@
         ffn_gain.reshape(1, 8),
         gate_proj,
         up_proj,
-        down_proj,
+        down_proj.T,
     )
     made = pl.pallas_call(
         spread_kernel,
@@ -918,13 +1029,12 @@
             jax.ShapeDtypeStruct((1, 8), f32),
             jax.ShapeDtypeStruct(gate_proj.shape, f32),
             jax.ShapeDtypeStruct(up_proj.shape, f32),
-            jax.ShapeDtypeStruct(down_proj.shape, f32),
+            jax.ShapeDtypeStruct(down_proj.shape[::-1], f32),
         ),
-        in_specs=[in_vmem] * 6,
-        out_specs=(in_vmem,) * 10,
+        grid=(1,),
         compiler_params=pltpu.CompilerParams(vmem_limit_bytes=16 * 1024 * 1024),
     )(*raw)
-    return (*made[:2], made[2].reshape(8), *made[3:6], made[6].reshape(8), *made[7:])
+    return (*made[:2], made[2].reshape(8), *made[3:6], made[6].reshape(8), *made[7:9], made[9].T)
 
 
 def solution(mesh):

time: 147 us -> 126 us (0.86)
  Pallas kernels: 138 us -> 120 us
  local copies, waits for them, and re-layouts: 7.81 us -> 5.33 us
    pallas_call x1, Pallas kernels: 136 us -> 118 us  [per_device(): pl.pallas_call(block_kernel, out_shape=out_shape, in_specs=[anywhere] * 1...]
    unnamed x14 -> x12, local copies, waits for them, and re-layouts: 7.81 us -> 5.33 us
where the time goes in v3:
time: 126 us
  Pallas kernels  120 us (95%)
  local copies, waits for them, and re-layouts  5.33 us (4%)
    pallas_call x1, Pallas kernels, per_device(): pl.pallas_call(block_kernel, out_shape=out_shape, in_specs=[anywhere] * 1...  118 us
    unnamed x12, local copies, waits for them, and re-layouts  5.33 us

profile of v3, /device:TPU:1, one launch (start us, length us, event | category | flops | bytes accessed | tf_op | source)
XLA Modules:
  0.0 125.5 jit_solution(14073670607979025663)
XLA Ops:
  0.6 118.0 %shard_map.177 = (bf16[128,1024]{1,0:T(8,128)(2,1)}, f32[128,1024]{1,0:T(8,128)}, f32[64,1792]{1,0:T(8,128)}, f32[8,8,384]{2,1,0:T(8,128)}, f32[64,128]{1,0:T(8,128)}, /*index=5*/f32[8,128]{1,0:T(8,128)}) custom-call(bf16[1,128,1024]{2,1,0:T(8,128)(2,1)} %x_hbm.1, bf16[1,128,1024]{2,1,0:T(8,128)(2,1)} %cot_hbm.1, bf16[1,8]{1,0:T(2,128)(2,1)} %bitcast.7, ...), custom_call_target="tpu_custom_call" | custom-call | tf_op jit(solution)/shard_map/pallas_call | solution.py:999
  118.7 0.0 copy-start.5
  118.7 0.7 copy-done.5
  119.4 0.0 copy-start
  119.4 1.0 copy-done
  120.4 0.0 copy-start.1
  120.4 1.0 copy-done.1
  121.4 0.0 copy-start.2
  121.4 0.9 copy-done.2
  122.4 0.0 copy-start.3
  122.4 0.9 copy-done.3
  123.3 0.0 copy-start.4
  123.3 0.8 copy-done.4
  124.0 1.5 %shard_map.178 = (bf16[1,128,1024]{2,1,0:T(8,128)(2,1)}, f32[1,128,1024]{2,1,0:T(8,128)}, f32[1,8]{1,0:T(1,128)}, f32[8,3072]{1,0:T(8,128)}, f32[3,8]{1,0:T(4,12...) custom-call(bf16[128,1024]{1,0:T(8,128)(2,1)S(1)} %copy-done.2, ...), custom_call_target="tpu_custom_call" | custom-call | tf_op jit(solution)/shard_map/pallas_call | solution.py:1020
Async XLA Ops:
  118.7 0.7 copy-start.5
  119.4 1.0 copy-start
  120.4 1.0 copy-start.1
  121.4 0.9 copy-start.2
  122.4 0.9 copy-start.3
  123.3 0.8 copy-start.4

commit v4 on v3

--- a/solution.py
+++ b/solution.py
@@ -13,8 +13,6 @@
 GU = 1152
 FFL = 1792
 HID = 640
-CR = 80
-CL = 512
 
 
 def mm(a, b):
@@ -79,50 +77,57 @@
 class RingGather:
     def __init__(self, link, view, me, plus, minus):
         self.link, self.view, self.me, self.plus, self.minus = link, view, me, plus, minus
+        self.left, self.far, self.right = ring(me, 3), ring(me, 2), ring(me, 1)
 
     def start(self):
-        own = self.view(self.me, None)
-        self.hp = self.link.send(own, own, self.plus)
-        self.hm = self.link.send(own, own, self.minus)
+        send = self.link.send
+        lo, hi = self.view(self.me, 0), self.view(self.me, 1)
+        self.p0, self.m1 = send(lo, lo, self.plus), send(hi, hi, self.minus)
+        self.p1, self.m0 = send(hi, hi, self.plus), send(lo, lo, self.minus)
 
     def forward(self):
-        left, right = ring(self.me, 3), ring(self.me, 1)
-        self.link.landed(self.hp, self.view(left, None))
-        part = self.view(left, 0)
+        part = self.view(self.left, 0)
+        self.link.landed(self.p0, part)
         self.fp = self.link.send(part, part, self.plus)
-        self.link.landed(self.hm, self.view(right, None))
-        part = self.view(right, 1)
+        part = self.view(self.right, 1)
+        self.link.landed(self.m1, part)
         self.fm = self.link.send(part, part, self.minus)
 
     def finish(self):
-        far = ring(self.me, 2)
-        self.link.landed(self.fp, self.view(far, 0))
-        self.link.landed(self.fm, self.view(far, 1))
+        self.link.landed(self.p1, self.view(self.left, 1))
+        self.link.landed(self.m0, self.view(self.right, 0))
+        self.link.landed(self.fp, self.view(self.far, 0))
+        self.link.landed(self.fm, self.view(self.far, 1))
 
 
 class RingScatter:
     def __init__(self, link, view, me, plus, minus, r1a, r1b, r2a, r2b):
         self.link, self.view, self.me, self.plus, self.minus = link, view, me, plus, minus
         self.r1a, self.r1b, self.r2a, self.r2b = r1a, r1b, r2a, r2b
+        self.left, self.far, self.right = ring(me, 3), ring(me, 2), ring(me, 1)
 
     def start(self):
-        far = ring(self.me, 2)
-        self.h1a = self.link.send(self.view(far, 0), self.r1a, self.plus)
-        self.h1b = self.link.send(self.view(far, 1), self.r1b, self.minus)
+        send = self.link.send
+        self.h1a = send(self.view(self.far, 0), self.r1a, self.plus)
+        self.h1b = send(self.view(self.far, 1), self.r1b, self.minus)
+        self.h2a1 = send(self.view(self.right, 1), self.r2a[1], self.plus)
+        self.h2b0 = send(self.view(self.left, 0), self.r2b[0], self.minus)
 
     def middle(self):
-        left, right = ring(self.me, 3), ring(self.me, 1)
         self.link.landed(self.h1a, self.r1a)
-        add_into(self.view(right, 0), self.r1a)
-        self.h2a = self.link.send(self.view(right, None), self.r2a, self.plus)
+        add_into(self.view(self.right, 0), self.r1a)
+        self.h2a0 = self.link.send(self.view(self.right, 0), self.r2a[0], self.plus)
         self.link.landed(self.h1b, self.r1b)
-        add_into(self.view(left, 1), self.r1b)
-        self.h2b = self.link.send(self.view(left, None), self.r2b, self.minus)
+        add_into(self.view(self.left, 1), self.r1b)
+        self.h2b1 = self.link.send(self.view(self.left, 1), self.r2b[1], self.minus)
 
     def finish(self):
-        self.link.landed(self.h2a, self.r2a)
-        self.link.landed(self.h2b, self.r2b)
-        add_into(self.view(self.me, None), self.r2a, self.r2b)
+        self.link.landed(self.h2a1, self.r2a[1])
+        self.link.landed(self.h2b0, self.r2b[0])
+        self.link.landed(self.h2a0, self.r2a[0])
+        self.link.landed(self.h2b1, self.r2b[1])
+        for part in (0, 1):
+            add_into(self.view(self.me, part), self.r2a[part], self.r2b[part])
 
 
 class DirectGather:
@@ -201,8 +206,12 @@
     def finish_near(self):
         self.link.landed(self.near, self.buf.at[self.y, self.mate])
 
+    def finish_sides(self):
+        for handle, ref in self.late[:4]:
+            self.link.landed(handle, ref)
+
     def finish_far(self):
-        for handle, ref in self.late:
+        for handle, ref in self.late[4:]:
             self.link.landed(handle, ref)
 
 
@@ -214,11 +223,11 @@
         self.left, self.far, self.right = ring(y, 3), ring(y, 2), ring(y, 1)
         self.mate = 1 - core
         self.first = link.reserve(4)
-        self.at_far, self.at_left, self.at_right, self.at_own = (1, 2, 3, 0) if own_first else (0, 1, 2, 3)
+        self.at_far, self.at_left, self.at_right, self.at_own = (2, 1, 3, 0) if own_first else (0, 1, 2, 3)
 
     def group(self, step):
         if self.own_first:
-            return lax.rem(self.y + 2 * step - step // 2, 4)
+            return lax.rem(self.y + 3 * step, 4)
         return lax.rem(self.y + 2 + step + step // 2 + 2 * (step // 3), 4)
 
     def cross(self, step):
@@ -242,11 +251,14 @@
         add_into(self.block(far, HI), self.rb.at[far, HI])
         self.h1b = self.link.send(self.block(far, HI), self.r1.at[1], self.minus)
 
-    def sides(self):
-        left, right = self.left, self.right
+    def side_left(self):
+        left = self.left
         self.crossed(left, self.at_left)
         add_into(self.block(left, LO), self.rb.at[left, LO])
         self.h2b0 = self.link.send(self.block(left, LO), self.r2.at[1, LO], self.minus)
+
+    def side_right(self):
+        right = self.right
         self.crossed(right, self.at_right)
         add_into(self.block(right, HI), self.rb.at[right, HI])
         self.h2a1 = self.link.send(self.block(right, HI), self.r2.at[0, HI], self.plus)
@@ -339,10 +351,11 @@
     h2g,
     dg,
     wf,
-    wc,
+    wi,
+    wp,
+    wo,
     pre_in,
     pre_pack,
-    w_in,
     wog,
     h1g,
     scale_g,
@@ -363,7 +376,9 @@
     rs_r1,
     rs_r2,
     gf,
-    gc,
+    gi,
+    gp,
+    go,
     gf_a1,
     gf_a2,
     gf_b1,
@@ -372,10 +387,12 @@
     gf_a4,
     gf_b3,
     gf_b4,
-    gc_r1,
-    gc_r2,
-    gc_r3,
-    gc_r4,
+    gi_r1,
+    gi_r2,
+    gp_r1,
+    gp_r2,
+    go_r1,
+    go_r2,
     post_send,
     post_in,
     post_own,
@@ -479,25 +496,38 @@
             RingGather(link, lambda i, p: buf.at[pair(p), i, :, b], x, x_plus, x_minus),
         )
 
-    def conv_gather(buf):
-        a, b = pl.ds(0, 256), pl.ds(256, 256)
+    low, high = pl.ds(0, 32), pl.ds(32, 32)
+
+    def in_gather():
         return (
-            DirectGather(link, lambda i, p: buf.at[z, i, :, a], x, along_x),
-            DirectGather(link, lambda i, p: buf.at[i, x, :, b], z, along_z),
-            DirectGather(link, lambda i, p: buf.at[i, :, :, a], z, along_z),
-            DirectGather(link, lambda i, p: buf.at[:, i, :, b], x, along_x),
-        )
-
-    def conv_scatter(buf, r1, r2, r3, r4):
-        a, b, o = pl.ds(0, 256), pl.ds(256, 128), pl.ds(384, 128)
-        rows = pl.ds(0, 64)
+            DirectGather(link, lambda i, p: wi.at[z, i, low], x, along_x),
+            DirectGather(link, lambda i, p: wi.at[i, x, high], z, along_z),
+            DirectGather(link, lambda i, p: wp.at[z, i], x, along_x),
+            DirectGather(link, lambda i, p: wi.at[i, :, low], z, along_z),
+            DirectGather(link, lambda i, p: wi.at[:, i, high], x, along_x),
+            DirectGather(link, lambda i, p: wp.at[i], z, along_z),
+        )
+
+    def out_gather():
         return (
-            DirectScatter(link, lambda i, p: buf.at[i, :, :, a], z, along_z, r1),
-            DirectScatter(link, lambda i, p: buf.at[:, i, rows, b], x, along_x, r2.at[0]),
-            DirectScatter(link, lambda i, p: buf.at[z, i, :, a], x, along_x, r3),
-            DirectScatter(link, lambda i, p: buf.at[i, x, rows, b], z, along_z, r4.at[0]),
-            DirectScatter(link, lambda i, p: buf.at[:, i, rows, o], x, along_x, r2.at[1]),
-            DirectScatter(link, lambda i, p: buf.at[i, x, rows, o], z, along_z, r4.at[1]),
+            DirectGather(link, lambda i, p: wo.at[i, x], z, along_z),
+            DirectGather(link, lambda i, p: wo.at[:, i], x, along_x),
+        )
+
+    def in_scatter():
+        return (
+            DirectScatter(link, lambda i, p: gi.at[i, :, low], z, along_z, gi_r1.at[0]),
+            DirectScatter(link, lambda i, p: gi.at[:, i, high], x, along_x, gi_r1.at[1]),
+            DirectScatter(link, lambda i, p: gp.at[i], z, along_z, gp_r1),
+            DirectScatter(link, lambda i, p: gi.at[z, i, low], x, along_x, gi_r2.at[0]),
+            DirectScatter(link, lambda i, p: gi.at[i, x, high], z, along_z, gi_r2.at[1]),
+            DirectScatter(link, lambda i, p: gp.at[z, i], x, along_x, gp_r2),
+        )
+
+    def out_scatter():
+        return (
+            DirectScatter(link, lambda i, p: go.at[:, i], x, along_x, go_r1),
+            DirectScatter(link, lambda i, p: go.at[i, x], z, along_z, go_r2),
         )
 
     def weight_scatter(buf, half, low, a1, a2, b1, b2, a3, a4, b3, b4):
@@ -511,16 +541,15 @@
         def pair(part):
             return pl.ds(0, 4) if part is None else pl.ds(2 * part, 2)
 
-        cut = (pl.ds(0, low), pl.ds(low, rows - low))
         return (
             RingScatter(link, lambda i, p: buf.at[i, pair(p), :, a], z, z_plus, z_minus,
-                        a1.at[0], a1.at[1], a2.at[0], a2.at[1]),
+                        a1.at[0], a1.at[1], (a2.at[0], a2.at[1]), (a2.at[2], a2.at[3])),
             RingScatter(link, lambda i, p: buf.at[pair(p), i, :, b], x, x_plus, x_minus,
-                        b1.at[0], b1.at[1], b2.at[0], b2.at[1]),
+                        b1.at[0], b1.at[1], (b2.at[0], b2.at[1]), (b2.at[2], b2.at[3])),
             RingScatter(link, lambda i, p: buf.at[z, i, rows_of(p), a], x, x_plus, x_minus,
-                        a3.at[cut[0]], a3.at[cut[1]], a4.at[0], a4.at[1]),
+                        a3.at[0], a3.at[1], (a4.at[0], a4.at[1]), (a4.at[2], a4.at[3])),
             RingScatter(link, lambda i, p: buf.at[i, x, rows_of(p), b], z, z_plus, z_minus,
-                        b3.at[cut[0]], b3.at[cut[1]], b4.at[0], b4.at[1]),
+                        b3.at[0], b3.at[1], (b4.at[0], b4.at[1]), (b4.at[2], b4.at[3])),
         )
 
     pre = []
@@ -533,53 +562,61 @@
         )
     gather_x = ctx_gather(xg)
     gather_x.start()
-    for load in loads[5:]:
+    for load in loads[5:6]:
+        load.wait()
+    out_rows = proj_ref[...].astype(f32)
+    wo[z, x] = jnp.concatenate(
+        [out_rows[:, 128 * w : 128 * w + 128] for w in range(8)], 0
+    ).astype(bf16)
+    out_w = out_gather()
+    out_w[0].start()
+    for load in loads[6:]:
         load.wait()
     own = wf.at[z, x]
     own[:, 0:512] = gate_ref[:, 0:512]
     own[:, 512:1024] = up_ref[:, 0:512]
     own[:, 1024:1152] = jnp.concatenate([gate_ref[:, 512:576], up_ref[:, 512:576]], 1)
-    own[:, 1152:1792] = jnp.concatenate(
-        [down_ref[...], jnp.zeros((64, 64), bf16)], 1
-    )
-    cotg[y, core] = cot_ref[0]
-    out_rows = proj_ref[...].astype(f32)
-    wc[z, x, 0:64, 384:512] = jnp.concatenate(
-        [out_rows[:, 128 * w : 128 * w + 128] for w in range(8)], 0
-    ).astype(bf16)
-    wc[z, x, 64:80, 128:512] = jnp.zeros((16, 384), bf16)
-    conv_w = conv_gather(wc)
+    own[:, 1152:1792] = jnp.concatenate([down_ref[...], jnp.zeros((64, 64), bf16)], 1)
     ffn_w = weight_gather(wf, 896, 32)
     for step, (h_in, h_pack) in enumerate(pre):
         link.landed(h_in, pre_in.at[lax.rem(c + 7 - step, 8)])
         link.landed(h_pack, pre_pack.at[step])
-    wc[z, x, 0:64, 0:384] = pre_in[...].reshape(64, 384).astype(bf16)
+    wi[z, x] = pre_in[...].reshape(64, 384).astype(bf16)
     summed = own_pack
     for step in range(7):
         summed = summed + pre_pack[step]
     tile = jnp.where(row < 2, summed, own_pack)
-    wc[z, x, 64:80, 0:128] = jnp.concatenate([tile, jnp.zeros_like(tile)], 0).astype(bf16)
-    conv_w[0].start()
-    conv_w[1].start()
-    gather_x.forward()
+    wp[z, x] = jnp.concatenate([tile, jnp.zeros_like(tile)], 0).astype(bf16)
+    in_w = in_gather()
+    for part in in_w[0:3]:
+        part.start()
     ffn_w[0].start()
     ffn_w[1].start()
+    out_w[0].finish()
+    out_w[1].start()
+    gather_x.forward()
+    for part in in_w[0:3]:
+        part.finish()
+    for part in in_w[3:6]:
+        part.start()
     gather_x.sides()
-    conv_w[0].finish()
-    conv_w[1].finish()
-    conv_w[2].start()
-    conv_w[3].start()
-    gather_x.across()
+    cotg[y, core] = cot_ref[0]
+    out_w[1].finish()
+    slab = wo[...].astype(f32).reshape(16, 8, 8, 128)
+    for w in range(8):
+        wog[y, core, :, 128 * w : 128 * w + 128] = slab[:, w].reshape(128, 128).astype(bf16)
+    gather_out = ctx_gather(wog)
+    gather_out.start()
     ffn_w[0].forward()
     ffn_w[1].forward()
-    gather_x.finish_near()
-    gather_x.finish_far()
-    gather_cot = ctx_gather(cotg)
-    gather_cot.start()
+    gather_x.across()
     ffn_w[0].finish()
     ffn_w[1].finish()
     ffn_w[2].start()
     ffn_w[3].start()
+    gather_x.finish_near()
+    gather_x.finish_sides()
+    gather_x.finish_far()
 
     def first_scale(g, carry):
         values = xg[g].reshape(256, 1024).astype(f32)
@@ -587,28 +624,25 @@
         return carry
 
     lax.fori_loop(0, 4, first_scale, 0)
-    conv_w[2].finish()
-    conv_w[3].finish()
-
-    packs = [wc[i // 4, i % 4, 64:80, 0:128].astype(f32)[0:8] for i in range(16)]
+    for part in in_w[3:6]:
+        part.finish()
+    gather_out.forward()
+    gather_cot = ctx_gather(cotg)
+    gather_cot.start()
+
+    packs = [wp[i // 4, i % 4].astype(f32)[0:8] for i in range(16)]
     gain_one = jnp.concatenate([packs[2 * w][0:1] + packs[2 * w + 1][0:1] for w in range(8)], 1)
     gain_two = jnp.concatenate([packs[2 * w][1:2] + packs[2 * w + 1][1:2] for w in range(8)], 1)
     taps = packs[0]
     for i in range(1, 16):
         taps = taps + packs[i]
     tap = [taps[2 + k : 3 + k] for k in range(3)]
-    w_in[...] = wc[:, :, 0:64, 0:384].reshape(1024, 384)
-    slab = wc[:, :, 0:64, 384:512].astype(f32).reshape(16, 8, 8, 128)
-    for w in range(8):
-        wog[y, core, :, 128 * w : 128 * w + 128] = slab[:, w].reshape(128, 128).astype(bf16)
-    gather_out = ctx_gather(wog)
-    gather_out.start()
 
     def project(g, carry):
         values = xg[g].reshape(256, 1024).astype(f32)
         lifted = (values * scale_g[g] * gain_one).astype(bf16)
         h1g[g] = lifted
-        proj[g] = mm(lifted, w_in[...])
+        proj[g] = mm(lifted, wi[...].reshape(1024, 384))
         return carry
 
     lax.fori_loop(0, 4, project, 0)
@@ -621,16 +655,14 @@
     y_buf[...] = (proj[:, :, 128:256].reshape(1024, 128) * z_all).astype(bf16).reshape(8, 128, 128)
     swap_y = exchange(y_buf, y_own)
     y_own[c] = y_buf[c]
-    gather_cot.forward()
-    gather_out.forward()
-    gather_cot.sides()
-    gather_out.sides()
-    gather_cot.across()
-    gather_out.across()
     ffn_w[2].forward()
     ffn_w[3].forward()
+    gather_out.sides()
+    gather_out.across()
+    gather_cot.forward()
     exchanged(swap_y, y_own)
     gather_out.finish_near()
+    gather_out.finish_sides()
     gather_out.finish_far()
     gated = jnp.concatenate([y_own[i] for i in range(8)], 1)
     middle = x_ref[0].astype(f32) + mm(gated, wog[...].reshape(1024, 1024))
@@ -638,7 +670,10 @@
     h2g[y, core] = (middle * scale_two * gain_two).astype(bf16)
     gather_h2 = ctx_gather(h2g)
     gather_h2.start()
+    gather_cot.sides()
+    gather_cot.across()
     gather_cot.finish_near()
+    gather_cot.finish_sides()
     gather_cot.finish_far()
     ffn_w[2].finish()
     ffn_w[3].finish()
@@ -654,10 +689,15 @@
         def _():
             gather_h2.forward()
             gather_h2.sides()
+            gather_h2.finish_sides()
+
+        @pl.when(step == 2)
+        def _():
+            scatter_dh2.side_left()
             gather_h2.across()
             gather_h2.finish_far()
 
-        @pl.when(step == 2)
+        @pl.when(step == 3)
         def _():
             scatter_dh2.start()
 
@@ -683,7 +723,7 @@
         return carry
 
     lax.fori_loop(0, 4, feed_forward, 0)
-    scatter_dh2.sides()
+    scatter_dh2.side_right()
     scatter_out = ctx_scatter(1)
 
     def ffn_out(step, carry):
@@ -696,7 +736,8 @@
     lax.fori_loop(0, 4, ffn_out, 0)
     scatter_dh2.middle()
     scatter_out.start()
-    scatter_out.sides()
+    scatter_out.side_left()
+    scatter_out.side_right()
 
     def grad_ffn(i, carry):
         lanes = pl.ds(pl.multiple_of(i * 256, 256), 256)
@@ -752,7 +793,7 @@
 
     def branch_back(step, carry):
         g = scatter_dh1.group(step)
-        d_lifted = mt(dp_buf[g], w_in[...])
+        d_lifted = mt(dp_buf[g], wi[...].reshape(1024, 384))
         rs_part[2, g] = d_lifted.astype(bf16).reshape(2, 128, 1024)
         scatter_dh1.cross(step)
         normed = xg[g].reshape(256, 1024).astype(f32) * scale_g[g]
@@ -761,46 +802,45 @@
 
     lax.fori_loop(0, 4, branch_back, 0)
     scatter_dh1.start()
-    scatter_dh1.sides()
+    scatter_dh1.side_left()
+    scatter_dh1.side_right()
 
     def grad_in(i, carry):
         lanes = pl.ds(pl.multiple_of(i * 256, 256), 256)
         lhs = h1g[:, :, lanes].reshape(1024, 256)
-        gc[i, :, 0:64, 0:384] = (
-            tm(lhs, dp_buf[...].reshape(1024, 384)).astype(bf16).reshape(4, 64, 384)
-        )
+        gi[i] = tm(lhs, dp_buf[...].reshape(1024, 384)).astype(bf16).reshape(4, 64, 384)
         return carry
 
     lax.fori_loop(0, 4, grad_in, 0)
     grad_mix = jnp.sum(mix_acc[...], axis=0, keepdims=True)
-    gc[:, :, 64:80, 128:512] = jnp.zeros((4, 4, 16, 384), bf16)
     for i in range(16):
         lanes = slice(128 * (i // 2), 128 * (i // 2) + 128)
         rows = [grad_mix[:, lanes], grad_gain_two[:, lanes], *grad_tap, jnp.zeros((11, 128), f32)]
-        gc[i // 4, i % 4, 64:80, 0:128] = jnp.concatenate(rows, 0).astype(bf16)
-    conv_g = conv_scatter(gc, gc_r1, gc_r2, gc_r3, gc_r4)
-    for part in conv_g[0:2]:
+        gp[i // 4, i % 4] = jnp.concatenate(rows, 0).astype(bf16)
+    in_g = in_scatter()
+    for part in in_g[0:3]:
         part.start()
     scatter_dh1.middle()
     gather_d.across()
     gather_d.finish_near()
+    gather_d.finish_sides()
     gather_d.finish_far()
     g_out = tm(y_buf[...].reshape(1024, 128), dg[...].reshape(1024, 1024))
     pieces = [g_out[:, 128 * w : 128 * w + 128].reshape(16, 1, 8, 128) for w in range(8)]
-    g_slab = jnp.concatenate(pieces, 1).reshape(4, 4, 64, 128)
-    gc[:, :, 0:64, 384:512] = g_slab.astype(bf16)
-    conv_g[4].start()
+    go[...] = jnp.concatenate(pieces, 1).reshape(4, 4, 64, 128).astype(bf16)
+    out_g = out_scatter()
+    out_g[0].start()
+    for part in in_g[0:3]:
+        part.finish()
+    for part in in_g[3:6]:
+        part.start()
     ffn_g[0].finish()
     ffn_g[1].finish()
     ffn_g[2].start()
     ffn_g[3].start()
-    for part in conv_g[0:2]:
-        part.finish()
-    for part in conv_g[2:4]:
-        part.start()
     scatter_out.middle()
-    conv_g[4].finish()
-    conv_g[5].start()
+    out_g[0].finish()
+    out_g[1].start()
 
     d_lifted = scatter_dh1.finish()
     local = x_ref[0].astype(f32)
@@ -826,12 +866,11 @@
     stores[0].start()
     ffn_g[2].middle()
     ffn_g[3].middle()
-    for part in conv_g[2:4]:
+    for part in in_g[3:6]:
         part.finish()
 
-    total = gc[z, x, :, 0:384].astype(f32)
-    post_send[...] = total[0:64].reshape(8, 8, 384)
-    post_own[...] = total[64:72, 0:128]
+    post_send[...] = gi[z, x].astype(f32).reshape(8, 8, 384)
+    post_own[...] = gp[z, x].astype(f32)[0:8]
     post = []
     for step, mate in enumerate(mates):
         post.append(
@@ -846,8 +885,8 @@
     stores[1].start()
     out_ref[...] = (middle + scatter_out.finish()).astype(bf16)
     stores[2].start()
-    conv_g[5].finish()
-    gwout_ref[...] = gc[z, x, 0:64, 384:512].astype(f32)
+    out_g[1].finish()
+    gwout_ref[...] = go[z, x].astype(f32)
     stores[3].start()
     post_in[c] = post_send[c]
     summed = post_own[...]
@@ -954,10 +993,11 @@
         v((4, 2, 128, 1024), bf16),
         v((4, 2, 128, 1024), bf16),
         v((4, 4, 64, FFL), bf16),
-        v((4, 4, CR, CL), bf16),
+        v((4, 4, 64, 384), bf16),
+        v((4, 4, 16, 128), bf16),
+        v((4, 4, 64, 128), bf16),
         v((8, 8, 384), f32),
         v((7, 8, 128), f32),
-        v((1024, 384), bf16),
         v((4, 2, 128, 1024), bf16),
         v((4, 256, 1024), bf16),
         v((4, 256, 1), f32),
@@ -978,19 +1018,23 @@
         v((3, 2, 64, 1024), bf16),
         v((3, 2, 128, 1024), bf16),
         v((4, 4, 64, FFL), bf16),
-        v((4, 4, CR, CL), bf16),
+        v((4, 4, 64, 384), bf16),
+        v((4, 4, 16, 128), bf16),
+        v((4, 4, 64, 128), bf16),
         v((2, 2, 64, 896), bf16),
-        v((2, 4, 64, 896), bf16),
+        v((4, 2, 64, 896), bf16),
         v((2, 2, 64, 896), bf16),
-        v((2, 4, 64, 896), bf16),
-        v((64, 896), bf16),
-        v((2, 64, 896), bf16),
-        v((64, 896), bf16),
-        v((2, 64, 896), bf16),
-        v((3, 4, CR, 256), bf16),
-        v((2, 3, 4, 64, 128), bf16),
-        v((3, CR, 256), bf16),
-        v((2, 3, 64, 128), bf16),
+        v((4, 2, 64, 896), bf16),
+        v((2, 32, 896), bf16),
+        v((4, 32, 896), bf16),
+        v((2, 32, 896), bf16),
+        v((4, 32, 896), bf16),
+        v((2, 3, 4, 32, 384), bf16),
+        v((2, 3, 32, 384), bf16),
+        v((3, 4, 16, 128), bf16),
+        v((3, 16, 128), bf16),
+        v((3, 4, 64, 128), bf16),
+        v((3, 64, 128), bf16),
         v((8, 8, 384), f32),
         v((8, 8, 384), f32),
         v((8, 128), f32),
@@ -1032,7 +1076,7 @@
             jax.ShapeDtypeStruct(down_proj.shape[::-1], f32),
         ),
         grid=(1,),
-        compiler_params=pltpu.CompilerParams(vmem_limit_bytes=16 * 1024 * 1024),
+        compiler_params=pltpu.CompilerParams(vmem_limit_bytes=62 * 1024 * 1024),
     )(*raw)
     return (*made[:2], made[2].reshape(8), *made[3:6], made[6].reshape(8), *made[7:9], made[9].T)
 

time: 126 us -> 117 us (0.929)
  local copies, waits for them, and re-layouts: 5.33 us -> 0 us
  Pallas kernels: 120 us -> 116 us
    unnamed x12 -> x0, local copies, waits for them, and re-layouts: 5.33 us -> none
    pallas_call x1, Pallas kernels: 118 us -> 114 us  [per_device(): pl.pallas_call(block_kernel, out_shape=out_shape, in_specs=[anywhere] * 1...]
    pallas_call x1, Pallas kernels: 1.5 us -> 2.79 us  [per_device(): pl.pallas_call(spread_kernel, out_shape=(jax.ShapeDtypeStruct(inputs.shap...]
where the time goes in v4:
time: 117 us
  Pallas kernels  116 us (99%)
    pallas_call x1, Pallas kernels, per_device(): pl.pallas_call(block_kernel, out_shape=out_shape, in_specs=[anywhere] * 1...  114 us
    pallas_call x1, Pallas kernels, per_device(): pl.pallas_call(spread_kernel, out_shape=(jax.ShapeDtypeStruct(inputs.shap...  2.79 us

profile of v4, /device:TPU:1, one launch (start us, length us, event | category | flops | bytes accessed | tf_op | source)
XLA Modules:
  0.0 117.2 jit_solution(5740144046325885032)
XLA Ops:
  0.6 113.6 %shard_map.177 = (bf16[128,1024]{1,0:T(8,128)(2,1)}, f32[128,1024]{1,0:T(8,128)}, f32[64,1792]{1,0:T(8,128)}, f32[8,8,384]{2,1,0:T(8,128)}, f32[64,128]{1,0:T(8,128)}, /*index=5*/f32[8,128]{1,0:T(8,128)}) custom-call(bf16[1,128,1024]{2,1,0:T(8,128)(2,1)} %x_hbm.1, bf16[1,128,1024]{2,1,0:T(8,128)(2,1)} %cot_hbm.1, bf16[1,8]{1,0:T(2,128)(2,1)} %bitcast.7, ...), custom_call_target="tpu_custom_call" | custom-call | tf_op jit(solution)/shard_map/pallas_call | solution.py:1043
  114.3 2.8 %shard_map.178 = (bf16[1,128,1024]{2,1,0:T(8,128)(2,1)}, f32[1,128,1024]{2,1,0:T(8,128)}, f32[1,8]{1,0:T(1,128)}, f32[8,3072]{1,0:T(8,128)}, f32[3,8]{1,0:T(4,12...) custom-call(bf16[128,1024]{1,0:T(8,128)(2,1)} %get-tuple-element.26.b, ...), custom_call_target="tpu_custom_call" | custom-call | tf_op jit(solution)/shard_map/pallas_call | solution.py:1064

commit v5 on v4

--- a/solution.py
+++ b/solution.py
@@ -355,7 +355,6 @@
     wp,
     wo,
     pre_in,
-    pre_pack,
     wog,
     h1g,
     scale_g,
@@ -395,8 +394,6 @@
     go_r2,
     post_send,
     post_in,
-    post_own,
-    post_pack,
 ):
     loads = [
         pltpu.make_async_copy(src, dst, local_sems.at[i])
@@ -456,7 +453,8 @@
     small = pack_ref[...]
     gains = pltpu.roll(small, 64 * lax.rem(f, 2) + 8 * c, 1)
     own_pack = jnp.where(row < 2, gains, pltpu.roll(small, 8 * f, 1))
-    pack_ref[...] = own_pack
+    for i in range(8):
+        win_ref[i, :, 384:512] = own_pack
     pre_in[c] = win_ref[c]
     pl.semaphore_wait(barrier, 13)
 
@@ -478,20 +476,16 @@
         for step, handle in enumerate(handles):
             link.landed(handle, landing.at[lax.rem(c + 7 - step, 8)])
 
-    def weight_gather(buf, half, low):
+    def weight_gather(buf, half):
         rest = buf.shape[3] - half
-        rows = buf.shape[2]
         a, b = pl.ds(0, half), pl.ds(half, rest)
-
-        def rows_of(part):
-            return pl.ds(0, rows) if part is None else (pl.ds(0, low), pl.ds(low, rows - low))[part]
 
         def pair(part):
             return pl.ds(0, 4) if part is None else pl.ds(2 * part, 2)
 
         return (
-            RingGather(link, lambda i, p: buf.at[z, i, rows_of(p), a], x, x_plus, x_minus),
-            RingGather(link, lambda i, p: buf.at[i, x, rows_of(p), b], z, z_plus, z_minus),
+            DirectGather(link, lambda i, p: buf.at[z, i, :, a], x, along_x),
+            DirectGather(link, lambda i, p: buf.at[i, x, :, b], z, along_z),
             RingGather(link, lambda i, p: buf.at[i, pair(p), :, a], z, z_plus, z_minus),
             RingGather(link, lambda i, p: buf.at[pair(p), i, :, b], x, x_plus, x_minus),
         )
@@ -552,14 +546,7 @@
                         b3.at[0], b3.at[1], (b4.at[0], b4.at[1]), (b4.at[2], b4.at[3])),
         )
 
-    pre = []
-    for step, mate in enumerate(mates):
-        pre.append(
-            (
-                link.send(win_ref.at[mate[1]], pre_in.at[c], mate),
-                link.send(pack_ref, pre_pack.at[step], mate),
-            )
-        )
+    pre = exchange(win_ref, pre_in)
     gather_x = ctx_gather(xg)
     gather_x.start()
     for load in loads[5:6]:
@@ -577,43 +564,36 @@
     own[:, 512:1024] = up_ref[:, 0:512]
     own[:, 1024:1152] = jnp.concatenate([gate_ref[:, 512:576], up_ref[:, 512:576]], 1)
     own[:, 1152:1792] = jnp.concatenate([down_ref[...], jnp.zeros((64, 64), bf16)], 1)
-    ffn_w = weight_gather(wf, 896, 32)
-    for step, (h_in, h_pack) in enumerate(pre):
-        link.landed(h_in, pre_in.at[lax.rem(c + 7 - step, 8)])
-        link.landed(h_pack, pre_pack.at[step])
-    wi[z, x] = pre_in[...].reshape(64, 384).astype(bf16)
-    summed = own_pack
-    for step in range(7):
-        summed = summed + pre_pack[step]
+    ffn_w = weight_gather(wf, 896)
+    ffn_w[0].start()
+    ffn_w[1].start()
+    cotg[y, core] = cot_ref[0]
+    out_w[0].finish()
+    out_w[1].start()
+    exchanged(pre, pre_in)
+    wi[z, x] = pre_in[:, :, 0:384].reshape(64, 384).astype(bf16)
+    summed = jnp.sum(pre_in[:, :, 384:512], axis=0)
     tile = jnp.where(row < 2, summed, own_pack)
     wp[z, x] = jnp.concatenate([tile, jnp.zeros_like(tile)], 0).astype(bf16)
     in_w = in_gather()
-    for part in in_w[0:3]:
+    for part in (in_w[2], in_w[0], in_w[1]):
         part.start()
-    ffn_w[0].start()
-    ffn_w[1].start()
-    out_w[0].finish()
-    out_w[1].start()
     gather_x.forward()
-    for part in in_w[0:3]:
-        part.finish()
-    for part in in_w[3:6]:
-        part.start()
-    gather_x.sides()
-    cotg[y, core] = cot_ref[0]
     out_w[1].finish()
     slab = wo[...].astype(f32).reshape(16, 8, 8, 128)
     for w in range(8):
         wog[y, core, :, 128 * w : 128 * w + 128] = slab[:, w].reshape(128, 128).astype(bf16)
     gather_out = ctx_gather(wog)
     gather_out.start()
-    ffn_w[0].forward()
-    ffn_w[1].forward()
+    for part, later in ((in_w[2], in_w[5]), (in_w[0], in_w[3]), (in_w[1], in_w[4])):
+        part.finish()
+        later.start()
+    ffn_w[0].finish()
+    ffn_w[2].start()
+    ffn_w[1].finish()
+    ffn_w[3].start()
+    gather_x.sides()
     gather_x.across()
-    ffn_w[0].finish()
-    ffn_w[1].finish()
-    ffn_w[2].start()
-    ffn_w[3].start()
     gather_x.finish_near()
     gather_x.finish_sides()
     gather_x.finish_far()
@@ -624,11 +604,7 @@
         return carry
 
     lax.fori_loop(0, 4, first_scale, 0)
-    for part in in_w[3:6]:
-        part.finish()
-    gather_out.forward()
-    gather_cot = ctx_gather(cotg)
-    gather_cot.start()
+    in_w[5].finish()
 
     packs = [wp[i // 4, i % 4].astype(f32)[0:8] for i in range(16)]
     gain_one = jnp.concatenate([packs[2 * w][0:1] + packs[2 * w + 1][0:1] for w in range(8)], 1)
@@ -638,14 +614,22 @@
         taps = taps + packs[i]
     tap = [taps[2 + k : 3 + k] for k in range(3)]
 
+    def lift(g, carry):
+        values = xg[g].reshape(256, 1024).astype(f32)
+        h1g[g] = (values * scale_g[g] * gain_one).astype(bf16)
+        return carry
+
     def project(g, carry):
-        values = xg[g].reshape(256, 1024).astype(f32)
-        lifted = (values * scale_g[g] * gain_one).astype(bf16)
-        h1g[g] = lifted
-        proj[g] = mm(lifted, wi[...].reshape(1024, 384))
+        proj[g] = mm(h1g[g], wi[...].reshape(1024, 384))
         return carry
 
+    lax.fori_loop(0, 4, lift, 0)
+    gather_out.forward()
+    in_w[3].finish()
+    in_w[4].finish()
     lax.fori_loop(0, 4, project, 0)
+    ffn_w[2].forward()
+    ffn_w[3].forward()
     b_part = proj[:, :, 0:128].reshape(1024, 128)
     x_part = proj[:, :, 256:384].reshape(1024, 128)
     bx_pad[0:8] = jnp.zeros((8, 128), f32)
@@ -655,11 +639,10 @@
     y_buf[...] = (proj[:, :, 128:256].reshape(1024, 128) * z_all).astype(bf16).reshape(8, 128, 128)
     swap_y = exchange(y_buf, y_own)
     y_own[c] = y_buf[c]
-    ffn_w[2].forward()
-    ffn_w[3].forward()
     gather_out.sides()
     gather_out.across()
-    gather_cot.forward()
+    gather_cot = ctx_gather(cotg)
+    gather_cot.start()
     exchanged(swap_y, y_own)
     gather_out.finish_near()
     gather_out.finish_sides()
@@ -670,14 +653,12 @@
     h2g[y, core] = (middle * scale_two * gain_two).astype(bf16)
     gather_h2 = ctx_gather(h2g)
     gather_h2.start()
-    gather_cot.sides()
-    gather_cot.across()
-    gather_cot.finish_near()
-    gather_cot.finish_sides()
-    gather_cot.finish_far()
+    gather_h2.forward()
+    gather_cot.forward()
     ffn_w[2].finish()
     ffn_w[3].finish()
     gather_h2.finish_near()
+    gather_cot.finish_near()
 
     scatter_dh2 = ctx_scatter(0, own_first=True)
     low_half = lax.broadcasted_iota(jnp.int32, (256, 128), 1) < 64
@@ -687,15 +668,18 @@
 
         @pl.when(step == 1)
         def _():
-            gather_h2.forward()
             gather_h2.sides()
+            gather_cot.sides()
             gather_h2.finish_sides()
+            gather_cot.finish_sides()
 
         @pl.when(step == 2)
         def _():
             scatter_dh2.side_left()
             gather_h2.across()
+            gather_cot.across()
             gather_h2.finish_far()
+            gather_cot.finish_far()
 
         @pl.when(step == 3)
         def _():
@@ -724,20 +708,6 @@
 
     lax.fori_loop(0, 4, feed_forward, 0)
     scatter_dh2.side_right()
-    scatter_out = ctx_scatter(1)
-
-    def ffn_out(step, carry):
-        g = scatter_out.group(step)
-        w_down = wf[:, :, :, GU:FFL].reshape(1024, HID)
-        rs_part[1, g] = mt(hid_buf[g], w_down).astype(bf16).reshape(2, 128, 1024)
-        scatter_out.cross(step)
-        return carry
-
-    lax.fori_loop(0, 4, ffn_out, 0)
-    scatter_dh2.middle()
-    scatter_out.start()
-    scatter_out.side_left()
-    scatter_out.side_right()
 
     def grad_ffn(i, carry):
         lanes = pl.ds(pl.multiple_of(i * 256, 256), 256)
@@ -747,9 +717,28 @@
         gf[i, :, :, GU:FFL] = (
             tm(lhs, hid_buf[...].reshape(1024, HID)).astype(bf16).reshape(4, 64, HID)
         )
+
+        @pl.when(i == 1)
+        def _():
+            scatter_dh2.middle()
+
         return carry
 
-    lax.fori_loop(0, 4, grad_ffn, 0)
+    lax.fori_loop(0, 2, grad_ffn, 0)
+    scatter_out = ctx_scatter(1)
+
+    def ffn_out(step, carry):
+        g = scatter_out.group(step)
+        w_down = wf[:, :, :, GU:FFL].reshape(1024, HID)
+        rs_part[1, g] = mt(hid_buf[g], w_down).astype(bf16).reshape(2, 128, 1024)
+        scatter_out.cross(step)
+        return carry
+
+    lax.fori_loop(0, 4, ffn_out, 0)
+    scatter_out.start()
+    scatter_out.side_left()
+    scatter_out.side_right()
+    lax.fori_loop(2, 4, grad_ffn, 0)
     ffn_g = weight_scatter(gf, 896, 32, gf_a1, gf_a2, gf_b1, gf_b2, gf_a3, gf_a4, gf_b3, gf_b4)
     ffn_g[0].start()
     ffn_g[1].start()
@@ -768,11 +757,12 @@
         dy_buf[i] = d_gated[:, 128 * i : 128 * i + 128]
     swap_dy = exchange(dy_buf, dy_own)
     gather_d = ctx_gather(dg)
+    dy_own[c] = dy_buf[c]
     gather_d.start()
-    dy_own[c] = dy_buf[c]
     ffn_g[0].middle()
     ffn_g[1].middle()
     exchanged(swap_dy, dy_own)
+    gather_d.forward()
 
     d_gated = dy_own[...].reshape(1024, 128).astype(f32)
     dz_pad[0:1024] = d_gated * proj[:, :, 128:256].reshape(1024, 128)
@@ -785,9 +775,16 @@
     grad_tap = [
         jnp.sum(dz_pad[0:1024] * bx_pad[6 + k : 1030 + k], axis=0, keepdims=True) for k in range(3)
     ]
-    gather_d.forward()
-    gather_d.sides()
-
+    def grad_in(i, carry):
+        lanes = pl.ds(pl.multiple_of(i * 256, 256), 256)
+        lhs = h1g[:, :, lanes].reshape(1024, 256)
+        gi[i] = tm(lhs, dp_buf[...].reshape(1024, 384)).astype(bf16).reshape(4, 64, 384)
+        return carry
+
+    lax.fori_loop(0, 4, grad_in, 0)
+    in_g = in_scatter()
+    in_g[0].start()
+    in_g[1].start()
     scatter_dh1 = ctx_scatter(2)
     mix_acc[...] = jnp.zeros((8, 1024), f32)
 
@@ -804,23 +801,17 @@
     scatter_dh1.start()
     scatter_dh1.side_left()
     scatter_dh1.side_right()
-
-    def grad_in(i, carry):
-        lanes = pl.ds(pl.multiple_of(i * 256, 256), 256)
-        lhs = h1g[:, :, lanes].reshape(1024, 256)
-        gi[i] = tm(lhs, dp_buf[...].reshape(1024, 384)).astype(bf16).reshape(4, 64, 384)
-        return carry
-
-    lax.fori_loop(0, 4, grad_in, 0)
     grad_mix = jnp.sum(mix_acc[...], axis=0, keepdims=True)
     for i in range(16):
         lanes = slice(128 * (i // 2), 128 * (i // 2) + 128)
         rows = [grad_mix[:, lanes], grad_gain_two[:, lanes], *grad_tap, jnp.zeros((11, 128), f32)]
         gp[i // 4, i % 4] = jnp.concatenate(rows, 0).astype(bf16)
-    in_g = in_scatter()
-    for part in in_g[0:3]:
-        part.start()
+    in_g[2].start()
+    for part, later in ((in_g[0], in_g[3]), (in_g[1], in_g[4]), (in_g[2], in_g[5])):
+        part.finish()
+        later.start()
     scatter_dh1.middle()
+    gather_d.sides()
     gather_d.across()
     gather_d.finish_near()
     gather_d.finish_sides()
@@ -830,17 +821,23 @@
     go[...] = jnp.concatenate(pieces, 1).reshape(4, 4, 64, 128).astype(bf16)
     out_g = out_scatter()
     out_g[0].start()
-    for part in in_g[0:3]:
-        part.finish()
-    for part in in_g[3:6]:
-        part.start()
+    scatter_out.middle()
     ffn_g[0].finish()
+    ffn_g[2].start()
     ffn_g[1].finish()
-    ffn_g[2].start()
     ffn_g[3].start()
-    scatter_out.middle()
     out_g[0].finish()
     out_g[1].start()
+    for part in in_g[3:6]:
+        part.finish()
+
+    post_send[:, :, 0:384] = gi[z, x].astype(f32).reshape(8, 8, 384)
+    own_pack = gp[z, x].astype(f32)[0:8]
+    for i in range(8):
+        post_send[i, :, 384:512] = own_pack
+    post = exchange(post_send, post_in)
+    ffn_g[2].middle()
+    ffn_g[3].middle()
 
     d_lifted = scatter_dh1.finish()
     local = x_ref[0].astype(f32)
@@ -864,21 +861,6 @@
         )
     ]
     stores[0].start()
-    ffn_g[2].middle()
-    ffn_g[3].middle()
-    for part in in_g[3:6]:
-        part.finish()
-
-    post_send[...] = gi[z, x].astype(f32).reshape(8, 8, 384)
-    post_own[...] = gp[z, x].astype(f32)[0:8]
-    post = []
-    for step, mate in enumerate(mates):
-        post.append(
-            (
-                link.send(post_send.at[mate[1]], post_in.at[c], mate),
-                link.send(post_own, post_pack.at[step], mate),
-            )
-        )
     ffn_g[2].finish()
     ffn_g[3].finish()
     gff_ref[...] = gf[z, x].astype(f32)
@@ -889,13 +871,10 @@
     gwout_ref[...] = go[z, x].astype(f32)
     stores[3].start()
     post_in[c] = post_send[c]
-    summed = post_own[...]
-    for step, (h_in, h_pack) in enumerate(post):
-        link.landed(h_in, post_in.at[lax.rem(c + 7 - step, 8)])
-        link.landed(h_pack, post_pack.at[step])
-        summed = summed + post_pack[step]
-    gwin_ref[...] = post_in[...]
-    gpack_ref[...] = jnp.where(row < 2, summed, post_own[...])
+    exchanged(post, post_in)
+    gwin_ref[...] = post_in[:, :, 0:384]
+    summed = jnp.sum(post_in[:, :, 384:512], axis=0)
+    gpack_ref[...] = jnp.where(row < 2, summed, own_pack)
     stores[4].start()
     stores[5].start()
     for store in stores:
@@ -986,7 +965,7 @@
         pltpu.SemaphoreType.DMA((16,)),
         pltpu.SemaphoreType.DMA((sems,)),
         pltpu.SemaphoreType.DMA((sems,)),
-        v((8, 8, 384), f32),
+        v((8, 8, 512), f32),
         v((8, 128), f32),
         v((4, 2, 128, 1024), bf16),
         v((4, 2, 128, 1024), bf16),
@@ -996,8 +975,7 @@
         v((4, 4, 64, 384), bf16),
         v((4, 4, 16, 128), bf16),
         v((4, 4, 64, 128), bf16),
-        v((8, 8, 384), f32),
-        v((7, 8, 128), f32),
+        v((8, 8, 512), f32),
         v((4, 2, 128, 1024), bf16),
         v((4, 256, 1024), bf16),
         v((4, 256, 1), f32),
@@ -1035,10 +1013,8 @@
         v((3, 16, 128), bf16),
         v((3, 4, 64, 128), bf16),
         v((3, 64, 128), bf16),
-        v((8, 8, 384), f32),
-        v((8, 8, 384), f32),
-        v((8, 128), f32),
-        v((7, 8, 128), f32),
+        v((8, 8, 512), f32),
+        v((8, 8, 512), f32),
     ]
     raw = pl.pallas_call(
         block_kernel,

time: 117 us -> 114 us (0.974)
  Pallas kernels: 116 us -> 113 us
    pallas_call x1, Pallas kernels: 114 us -> 110 us  [per_device(): pl.pallas_call(block_kernel, out_shape=out_shape, in_specs=[anywhere] * 1...]
where the time goes in v5:
time: 114 us; the launch traced here: 113 us
  Pallas kernels  113 us (99%)
    pallas_call x1, Pallas kernels, per_device(): pl.pallas_call(block_kernel, out_shape=out_shape, in_specs=[anywhere] * 1...  110 us
    pallas_call x1, Pallas kernels, per_device(): pl.pallas_call(spread_kernel, out_shape=(jax.ShapeDtypeStruct(inputs.shap...  2.79 us

profile of v5, /device:TPU:1, one launch (start us, length us, event | category | flops | bytes accessed | tf_op | source)
XLA Modules:
  0.0 113.4 jit_solution(541955402950001452)
XLA Ops:
  0.6 109.9 %shard_map.177 = (bf16[128,1024]{1,0:T(8,128)(2,1)}, f32[128,1024]{1,0:T(8,128)}, f32[64,1792]{1,0:T(8,128)}, f32[8,8,384]{2,1,0:T(8,128)}, f32[64,128]{1,0:T(8,128)}, /*index=5*/f32[8,128]{1,0:T(8,128)}) custom-call(bf16[1,128,1024]{2,1,0:T(8,128)(2,1)} %x_hbm.1, bf16[1,128,1024]{2,1,0:T(8,128)(2,1)} %cot_hbm.1, bf16[1,8]{1,0:T(2,128)(2,1)} %bitcast.7, ...), custom_call_target="tpu_custom_call" | custom-call | tf_op jit(solution)/shard_map/pallas_call | solution.py:1019
  110.5 2.8 %shard_map.178 = (bf16[1,128,1024]{2,1,0:T(8,128)(2,1)}, f32[1,128,1024]{2,1,0:T(8,128)}, f32[1,8]{1,0:T(1,128)}, f32[8,3072]{1,0:T(8,128)}, f32[3,8]{1,0:T(4,12...) custom-call(bf16[128,1024]{1,0:T(8,128)(2,1)} %get-tuple-element.26.b, ...), custom_call_target="tpu_custom_call" | custom-call | tf_op jit(solution)/shard_map/pallas_call | solution.py:1040

commit v6 on v5

--- a/solution.py
+++ b/solution.py
@@ -548,7 +548,6 @@
 
     pre = exchange(win_ref, pre_in)
     gather_x = ctx_gather(xg)
-    gather_x.start()
     for load in loads[5:6]:
         load.wait()
     out_rows = proj_ref[...].astype(f32)
@@ -571,6 +570,7 @@
     out_w[0].finish()
     out_w[1].start()
     exchanged(pre, pre_in)
+    gather_x.start()
     wi[z, x] = pre_in[:, :, 0:384].reshape(64, 384).astype(bf16)
     summed = jnp.sum(pre_in[:, :, 384:512], axis=0)
     tile = jnp.where(row < 2, summed, own_pack)

time: 114 us -> 113 us (level)
  no operation moved by 1% of the time
where the time goes in v6:
time: 113 us
  Pallas kernels  112 us (99%)
    pallas_call x1, Pallas kernels, per_device(): pl.pallas_call(block_kernel, out_shape=out_shape, in_specs=[anywhere] * 1...  109 us
    pallas_call x1, Pallas kernels, per_device(): pl.pallas_call(spread_kernel, out_shape=(jax.ShapeDtypeStruct(inputs.shap...  2.79 us

profile of v6, /device:TPU:1, one launch (start us, length us, event | category | flops | bytes accessed | tf_op | source)
XLA Modules:
  0.0 113.0 jit_solution(5313618239995270142)
XLA Ops:
  0.6 109.5 %shard_map.177 = (bf16[128,1024]{1,0:T(8,128)(2,1)}, f32[128,1024]{1,0:T(8,128)}, f32[64,1792]{1,0:T(8,128)}, f32[8,8,384]{2,1,0:T(8,128)}, f32[64,128]{1,0:T(8,128)}, /*index=5*/f32[8,128]{1,0:T(8,128)}) custom-call(bf16[1,128,1024]{2,1,0:T(8,128)(2,1)} %x_hbm.1, bf16[1,128,1024]{2,1,0:T(8,128)(2,1)} %cot_hbm.1, bf16[1,8]{1,0:T(2,128)(2,1)} %bitcast.7, ...), custom_call_target="tpu_custom_call" | custom-call | tf_op jit(solution)/shard_map/pallas_call | solution.py:1019
  110.1 2.8 %shard_map.178 = (bf16[1,128,1024]{2,1,0:T(8,128)(2,1)}, f32[1,128,1024]{2,1,0:T(8,128)}, f32[1,8]{1,0:T(1,128)}, f32[8,3072]{1,0:T(8,128)}, f32[3,8]{1,0:T(4,12...) custom-call(bf16[128,1024]{1,0:T(8,128)(2,1)} %get-tuple-element.26.b, ...), custom_call_target="tpu_custom_call" | custom-call | tf_op jit(solution)/shard_map/pallas_call | solution.py:1040
